TPU v7x, 128 devices: a whole 4x4x4 slice. The times are simulated.
128 devices in a mesh: row: 8 (over x_lo, z), col: 16 (over x_hi, y, core).
Axes of the slice: x: 4 (x_hi: 2, x_lo: 2; x = x_hi * 2 + x_lo), y: 4, z: 4, core: 2. Of those that a mesh axis runs over, the one named last changes fastest.
Arguments:
- inverse_block: float32 [12288, 12288], P('row', 'col'), may hold values from -0.14433757 to 0.14433757, as said below
- grid_position: int32 [12288], replicated, may hold values from 0 to 12287, each once
- panel_a: float32 [512, 12288], P('row', 'col'), may hold values from -1.5 to 1.5
- pivot_inverse_a: float32 [512, 512], replicated, may hold values from -6 to 6
- chosen_rows: int32 [8192], replicated, may hold values from 0 to 12287, as said below
- top_panel_b: float32 [512, 512], replicated, may hold values from -1.5 to 1.5
- panel_b: float32 [512, 8192], P('row', 'col'), may hold values from -1.5 to 1.5
- pivot_inverse_b: float32 [512, 512], replicated, may hold values from -6 to 6
Outputs:
- inverse_panel_a: float32 [12288, 512], P(('row', 'col'))
- diagonal_a: float32 [512, 512], replicated
- inverse_panel_b: float32 [12288, 512], P(('row', 'col'))
- inverse_top_b: float32 [512, 512], replicated
- diagonal_b: float32 [512, 512], replicated
Inputs may be any that keep to these rules, and one draw needn't show every extreme that they name: `grid_position`: each of 0 to 12287 appears once. `chosen_rows`: 8192 distinct values. `inverse_block`: symmetric: entry (i, j) equals entry (j, i) in grid storage order.
All inputs are finite; a program needn't handle non-finite values.
Results may differ from a plain program's by a relative error of at most 0.00008.
Values sent between devices are 32-bit elements; how exact they have to be, the bound alone decides.
A program may use at most 128 MiB of HBM per device.

v0:
```python
import jax
import jax.numpy as jnp
from jax import lax
from jax.sharding import PartitionSpec as P


def pick_columns(wide, index, limit):
    valid = (index < limit).astype(jnp.float32)
    taken = jnp.take(wide, jnp.minimum(index, limit - 1), axis=1)
    return taken * valid[None, :]


def select_columns(wide, source, start, length, limit):
    index = lax.dynamic_slice_in_dim(source, start, length, 0)
    return pick_columns(wide, index, limit)


def project(block, panel_t):
    return lax.dot_general(
        block,
        panel_t,
        (((1,), (1,)), ((), ())),
        precision=lax.Precision.HIGHEST,
        preferred_element_type=jnp.float32,
    )


def body(
    inverse_block,
    grid_position,
    panel_a,
    pivot_inverse_a,
    chosen_rows,
    top_panel_b,
    panel_b,
    pivot_inverse_b,
):
    exact = lax.Precision.HIGHEST
    rows_here = inverse_block.shape[0]
    cols_here = inverse_block.shape[1]
    order = grid_position.shape[0]
    count = chosen_rows.shape[0]
    row_count = lax.axis_size("row")
    own_rows = rows_here // lax.axis_size("col")
    col_start = lax.axis_index("col") * cols_here
    own_start = lax.axis_index("row") * rows_here + lax.axis_index("col") * own_rows
    group_starts = (
        jnp.arange(row_count, dtype=jnp.int32) * rows_here + lax.axis_index("col") * own_rows
    )
    group_index = (group_starts[:, None] + jnp.arange(own_rows, dtype=jnp.int32)[None, :]).reshape(
        -1
    )
    local_offset = lax.axis_index("row") * own_rows
    source_a = (
        jnp.zeros((order,), jnp.int32).at[grid_position].set(jnp.arange(order, dtype=jnp.int32))
    )
    source_b = (
        jnp.full((order,), count, jnp.int32)
        .at[grid_position[chosen_rows]]
        .set(jnp.arange(count, dtype=jnp.int32))
    )
    group_a = source_a[group_index]
    group_b = source_b[group_index]
    valid_own = (lax.dynamic_slice_in_dim(source_b, own_start, own_rows, 0) < count).astype(
        jnp.float32
    )
    wide_a = lax.all_gather(panel_a, "col", axis=1, tiled=True)
    cols_a, group_own_a = (
        lax.all_gather(
            select_columns(wide_a, source_a, col_start, cols_here, order), "row", axis=0, tiled=True
        ),
        lax.all_gather(pick_columns(wide_a, group_a, order), "row", axis=0, tiled=True),
    )
    product_a = lax.psum_scatter(
        project(inverse_block, cols_a), "col", scatter_dimension=0, tiled=True
    )
    wide_b = lax.all_gather(panel_b, "col", axis=1, tiled=True)
    cols_b, group_own_b = (
        lax.all_gather(
            select_columns(wide_b, source_b, col_start, cols_here, count), "row", axis=0, tiled=True
        ),
        lax.all_gather(pick_columns(wide_b, group_b, count), "row", axis=0, tiled=True),
    )
    product_b = lax.psum_scatter(
        project(inverse_block, cols_b), "col", scatter_dimension=0, tiled=True
    )
    own_a = lax.dynamic_slice_in_dim(group_own_a, local_offset, own_rows, 1)
    own_b = lax.dynamic_slice_in_dim(group_own_b, local_offset, own_rows, 1)
    inverse_panel_a = -product_a
    diag_part = jnp.dot(own_a, inverse_panel_a, precision=exact, preferred_element_type=jnp.float32)
    cross_part = lax.dot_general(
        inverse_panel_a,
        own_b,
        (((0,), (1,)), ((), ())),
        precision=exact,
        preferred_element_type=jnp.float32,
    )
    diag_total, cross = lax.psum((diag_part, cross_part), ("row", "col"))
    diagonal_a = pivot_inverse_a - diag_total
    inverse_top_b = -(
        jnp.dot(diagonal_a, top_panel_b, precision=exact, preferred_element_type=jnp.float32)
        + cross
    )
    bottom = product_b + jnp.dot(
        inverse_panel_a, top_panel_b, precision=exact, preferred_element_type=jnp.float32
    )
    inverse_panel_b = -bottom * valid_own[:, None]
    last_part = jnp.dot(own_b, inverse_panel_b, precision=exact, preferred_element_type=jnp.float32)
    last_total = lax.psum(last_part, ("row", "col"))
    diagonal_b = (
        pivot_inverse_b
        - jnp.dot(top_panel_b.T, inverse_top_b, precision=exact, preferred_element_type=jnp.float32)
        - last_total
    )
    return (inverse_panel_a, diagonal_a, inverse_panel_b, inverse_top_b, diagonal_b)


def solution(mesh):
    in_specs = (P("row", "col"), P(), P("row", "col"), P(), P(), P(), P("row", "col"), P())
    out_specs = (P(("row", "col"), None), P(), P(("row", "col"), None), P(), P())
    return jax.shard_map(body, mesh=mesh, in_specs=in_specs, out_specs=out_specs, check_vma=False)
```

profile of v0, /device:TPU:1, one launch (start us, length us, event | category | flops | bytes accessed | tf_op | source)
XLA Modules:
  0.0 630.4 jit_solution(11764547674448368654)
XLA Ops:
  11.9 45.4 %scatter_custom_fusion = s32[12288]{0:T(1024)S(1)} fusion(s32[12288]{0:T(1024)S(1)} %compare_select_fusion.1, s32[12288]{0:T(1024)S(1)} %iota.15, s32[]{:T(128)} %constant.4.clone.1), kind=kCustom, calls=%fused_computation.35 | custom fusion | bytes 49156 | tf_op jit(solution)/shard_map/scatter | solution.py:55
  57.4 21.3 %all-gather.7.cloned.1.call-done = f32[64,12288]{0,1:T(8,128)} async-done(((f32[64,768]{0,1:T(8,128)}), f32[64,12288]{0,1:T(8,128)}) %all-gather.7.cloned.1.call-update) | async-done | bytes 3145744 | tf_op jit(solution)/shard_map/all_gather | solution.py:67
  78.7 4.3 gather_fusion.3
  84.1 45.5 %gather_fusion.1 = s32[8192]{0:T(1024)S(1)} fusion(s32[12288]{0:T(1024)S(1)} %copy-done.1, s32[8192]{0:T(1024)S(1)} %fusion.11), kind=kCustom, calls=%fused_computation.5 | custom fusion | bytes 98304 | tf_op jit(solution)/shard_map/gather | solution.py:59
  129.7 30.5 %scatter_custom_fusion.1 = s32[12288]{0:T(1024)S(1)} fusion(s32[8192]{0:T(1024)S(1)} %bitcast.35, s32[8192]{0:T(1024)S(1)} %iota.17, s32[]{:T(128)} %constant.36.clone.1), kind=kCustom, calls=%fused_computation.33 | custom fusion | bytes 49156 | tf_op jit(solution)/shard_map/scatter | solution.py:60
  160.3 3.8 gather_fusion.5
  165.0 4.1 all-gather.9.cloned.1.call-done
  169.0 11.3 %convolution_bitcast_fusion.1 = f32[1536,512]{0,1:T(8,128)} fusion(f32[512,768]{1,0:T(8,128)} %all-gather.9.cloned.1.call-done, f32[1536,768]{1,0:T(8,128)} %param.12), kind=kOutput, calls=%fused_computation.10 | convolution fusion | flops 7247757312 | bytes 9437184 | tf_op jit(solution)/shard_map/dot_general | solution.py:19
  180.3 3.7 copy.52
  184.3 4.5 gather_fusion
  188.8 4.4 gather_fusion.4
  194.1 4.5 gather_fusion.2
  198.6 3.8 gather_fusion.6
  203.5 7.6 %all-gather.15.cloned.1.call-done = f32[512,768]{1,0:T(8,128)} async-done(((f32[64,768]{1,0:T(8,128)}), f32[512,768]{1,0:T(8,128)}) %all-gather.15.cloned.1.call-update) | async-done | bytes 1572880 | tf_op jit(solution)/shard_map/all_gather | solution.py:79
  211.0 11.3 %convolution_bitcast_fusion = f32[1536,512]{0,1:T(8,128)} fusion(f32[512,768]{1,0:T(8,128)} %all-gather.15.cloned.1.call-done, f32[1536,768]{1,0:T(8,128)} %param.12), kind=kOutput, calls=%fused_computation.9 | convolution fusion | flops 7247757312 | bytes 9437184 | tf_op jit(solution)/shard_map/dot_general | solution.py:19
  222.4 3.5 copy.54
  226.0 68.4 %reduce-scatter.7.cloned.1.call-done = f32[96,512]{1,0:T(8,128)} async-done(((f32[1536,512]{1,0:T(8,128)}), f32[96,512]{1,0:T(8,128)}) %reduce-scatter.7.cloned.1.call-update) | async-done | bytes 196624
  295.5 35.5 %all-gather.11.cloned.1.call-done = f32[512,768]{1,0:T(8,128)} async-done(((f32[64,768]{1,0:T(8,128)}), f32[512,768]{1,0:T(8,128)}) %all-gather.11.cloned.1.call-update) | async-done | bytes 1572880 | tf_op jit(solution)/shard_map/all_gather | solution.py:72
  331.1 3.0 fusion.5
  334.1 39.1 %all-gather.17.cloned.1.call-done = f32[512,768]{1,0:T(8,128)} async-done(((f32[64,768]{1,0:T(8,128)}), f32[512,768]{1,0:T(8,128)}) %all-gather.17.cloned.1.call-update) | async-done | bytes 1572880 | tf_op jit(solution)/shard_map/all_gather | solution.py:82
  373.2 3.1 fusion.9
  376.3 80.5 %reduce-scatter.9.cloned.1.call-done = f32[96,512]{1,0:T(8,128)} async-done(((f32[1536,512]{1,0:T(8,128)}), f32[96,512]{1,0:T(8,128)}) %reduce-scatter.9.cloned.1.call-update) | async-done | bytes 196624 | tf_op jit(solution)/shard_map/reduce_scatter | solution.py:84
  459.2 3.1 fusion.7
  466.4 149.7 %all-reduce.3.cloned.1.call-done = (f32[512,512]{1,0:T(8,128)}, f32[512,512]{1,0:T(8,128)}, f32[512,512]{0,1:T(8,128)}) async-done(((f32[512,512]{1,0:T(8,128)}, f32[512,512]{1,0:T(8,128)}, f32[512,512]{0,1:T(8,128)}), (f32[512,512]{1,0:T(8,128)}, f32[512,512]{1,0:T(8,128)}, f32[512,512]{0,1:T(8,128)})) %all-reduce.3.cloned.1.call-update) | async-done | bytes 3145744 | tf_op jit(solution)/shard_map/psum | solution.py:98
  (77 shorter events, 24.3 us)
Async XLA Ops:
  7.2 449.6 %copy-start = (f32[512,512]{1,0:T(8,128)S(1)}, f32[512,512]{1,0:T(8,128)}, u32[]{:S(2)}) copy-start(f32[512,512]{1,0:T(8,128)} %param.17) | copy-start | bytes 3145732
  7.2 76.9 %copy-start.1 = (s32[12288]{0:T(1024)S(1)}, s32[12288]{0:T(1024)}, u32[]{:S(2)}) copy-start(s32[12288]{0:T(1024)} %param.13) | copy-start | bytes 147460
  7.2 76.8 %copy-start.8 = (s32[8192]{0:T(1024)S(1)}, s32[8192]{0:T(1024)}, u32[]{:S(2)}) copy-start(s32[8192]{0:T(1024)} %param.16) | copy-start | bytes 98308
  7.2 71.5 %all-gather.7.cloned.1.call-start = ((), (), s32[]{:S(2)}) async-start(), calls=%async_computation.2 | async-start | bytes 6684672 | tf_op jit(solution)/shard_map/all_gather | solution.py:67
  9.2 151.1 %all-gather.13.cloned.1.call-start = ((), (), s32[]{:S(2)}) async-start(), calls=%async_computation.5 | async-start | bytes 4456448 | tf_op jit(solution)/shard_map/all_gather | solution.py:77
  11.0 158.0 %all-gather.9.cloned.1.call-start = ((), (), s32[]{:S(2)}) async-start(), calls=%async_computation.3 | async-start | bytes 1769472 | tf_op jit(solution)/shard_map/all_gather | solution.py:69
  84.0 127.1 %all-gather.15.cloned.1.call-start = ((), (), s32[]{:S(2)}) async-start(), calls=%async_computation.6 | async-start | bytes 1769472 | tf_op jit(solution)/shard_map/all_gather | solution.py:79
  164.9 129.5 %reduce-scatter.7.cloned.1.call-start = ((), (), s32[]{:S(2)}) async-start(), calls=%async_computation.8 | async-start | bytes 3342336
  184.0 147.1 %all-gather.11.cloned.1.call-start = ((), (), s32[]{:S(2)}) async-start(), calls=%async_computation.4 | async-start | bytes 1769472 | tf_op jit(solution)/shard_map/all_gather | solution.py:72
  194.0 179.2 %all-gather.17.cloned.1.call-start = ((), (), s32[]{:S(2)}) async-start(), calls=%async_computation.7 | async-start | bytes 1769472 | tf_op jit(solution)/shard_map/all_gather | solution.py:82
  203.3 253.5 %reduce-scatter.9.cloned.1.call-start = ((), (), s32[]{:S(2)}) async-start(), calls=%async_computation.9 | async-start | bytes 3342336 | tf_op jit(solution)/shard_map/reduce_scatter | solution.py:84
  225.9 390.2 %all-reduce.3.cloned.1.call-start = ((), (), s32[]{:S(2)}) async-start(), calls=%async_computation.10 | async-start | bytes 6291456 | tf_op jit(solution)/shard_map/psum | solution.py:98
  458.5 0.7 copy-start.7
  462.3 153.9 %copy-start.4 = (f32[512,512]{1,0:T(8,128)S(1)}, f32[512,512]{1,0:T(8,128)}, u32[]{:S(2)}) copy-start(f32[512,512]{1,0:T(8,128)} %param.15) | copy-start | bytes 3145732
  616.1 1.6 copy-start.6
  616.1 4.5 copy-start.5
  617.7 1.9 copy-start.2
  619.6 1.0 copy-start.3
Sparse Core Ops, SparseCore 0:
  11.1 67.6 all-gather.6
  81.8 53.0 all-gather.12
  137.1 31.9 all-gather.8
  171.1 39.8 all-gather.14
  214.9 79.4 reduce-scatter.6
  296.5 34.4 all-gather.10
  333.3 39.8 all-gather.16
  377.2 79.5 reduce-scatter.8
  462.5 153.5 all-reduce.2
where the time goes:
time: 631 us; the launch traced here: 630 us
  waiting for transfers between devices  406 us (64%)
  local copies, waits for them, and re-layouts  166 us (26%)
  matrix products  37.4 us (6%)
  between operations  14.2 us (2%)
  other arithmetic  6.35 us (1%)
    psum x1, waiting for transfers between devices, body(): diag_total, cross = lax.psum((diag_part, cross_part), ('row', 'col'))  150 us
    reduce_scatter x1, waiting for transfers between devices, body(): lax.psum_scatter(project(inverse_block, cols_b), 'col', scatter_dimension...  80.5 us
    unnamed x10, waiting for transfers between devices  68.6 us
    gather x1, local copies, waits for them, and re-layouts, body(): grid_position[chosen_rows]  45.5 us
    scatter x1, local copies, waits for them, and re-layouts, body(): jnp.zeros((order,), jnp.int32).at[grid_position]  45.4 us
    all_gather x1, waiting for transfers between devices, body(): lax.all_gather(pick_columns(wide_b, group_b, count), 'row', axis=0, tiled...  39.1 us
    all_gather x1, waiting for transfers between devices, body(): lax.all_gather(pick_columns(wide_a, group_a, order), 'row', axis=0, tiled...  35.5 us
    scatter x1, local copies, waits for them, and re-layouts, body(): source_b = jnp.full((order,), count, jnp.int32).at[grid_position[chosen_r...  30.5 us
  transfers between devices with their start and end apart: 9, of which 8 were waited for; matrix products, arithmetic and copies ran while one was open for 31% of the time, Pallas kernels for 0%

commit v1 on v0

v1 whole, which is shorter than its diff:
```python
import functools

import jax
import jax.numpy as jnp
from jax import lax
from jax.experimental import pallas as pl
from jax.experimental.pallas import tpu as pltpu
from jax.sharding import PartitionSpec as P

MESH = pl.DeviceIdType.MESH
F32 = jnp.float32
BF16 = jnp.bfloat16
NT = (((1,), (1,)), ((), ()))
W = 512
FEAT = 64
MA = 768
MB = 512
OWN = 96
COL_STEPS = ((0, 1), (0, 3), (0, 2), (1, 0), (1, 1), (1, 3), (1, 2))
ROW_STEPS = ((1, 0), (0, 1), (0, 3), (0, 2), (1, 1), (1, 3), (1, 2))


def split(x):
    high = x.astype(BF16)
    return high, (x - high.astype(F32)).astype(BF16)


def dot_nn(a, b):
    return jnp.dot(a, b, preferred_element_type=F32)


def dot_nt(a, b):
    return lax.dot_general(a, b, NT, preferred_element_type=F32)


def dot3(a, b):
    ah, al = split(a)
    bh, bl = split(b)
    return dot_nn(ah, bh) + (dot_nn(ah, bl) + dot_nn(al, bh))


def remote(src, dst, send, recv, device):
    return pltpu.make_async_remote_copy(
        src_ref=src,
        dst_ref=dst,
        send_sem=send,
        recv_sem=recv,
        device_id=device,
        device_id_type=MESH,
    )


def main_kernel(
    block_ref,
    gp_ref,
    gpt_ref,
    chosen_ref,
    pa_ref,
    pb_ref,
    out_pa_ref,
    out_pb_ref,
    out_sel_ref,
    out_g_ref,
    b_f32,
    b_high,
    b_low,
    gb,
    xa,
    xb,
    near,
    far,
    far_in,
    full,
    full_high,
    full_low,
    half_out,
    half_in,
    half_own,
    ring_in,
    own_out,
    own_in,
    gram,
    gram_core,
    gram_1,
    gram_2,
    gram_3,
    b_sem,
    y_send,
    y_recv,
    c_send,
    c_recv,
    far_send,
    far_recv,
    row_send,
    row_recv,
    half_send,
    half_recv,
    ring_send,
    ring_recv,
    own_send,
    own_recv,
    gc_send,
    gc_recv,
    gs_send,
    gs_recv,
    gg_send,
    gg_recv,
):
    r = lax.axis_index("row")
    c = lax.axis_index("col")
    x_lo, z = r // 4, r % 4
    x_hi, y, core = c // 8, (c // 2) % 4, c % 2
    x = x_hi * 2 + x_lo
    mate = (r, c + 1 - 2 * core)

    def col_device(dx, dy):
        return (r, (((x_hi + dx) % 2) * 4 + (y + dy) % 4) * 2 + core)

    def row_device(dx, dz):
        return (((x_lo + dx) % 2) * 4 + (z + dz) % 4, c)

    def x_device(dx):
        nx = (x + dx) % 4
        return ((nx % 2) * 4 + z, ((nx // 2) * 4 + y) * 2 + core)

    def y_device(dy):
        return col_device(0, dy)

    def z_device(dz):
        return row_device(0, dz)

    own_to = (c // 2, (c % 2) * 8 + r)
    own_from = (c % 8, 2 * r + c // 8)
    own_self = jnp.logical_and(own_to[0] == r, own_to[1] == c)

    block_copy = pltpu.make_async_copy(block_ref, b_f32, b_sem)
    block_copy.start()

    barrier = pltpu.get_barrier_semaphore()

    def greet(device):
        pl.semaphore_signal(barrier, inc=1, device_id=device, device_id_type=MESH)

    greet(mate)
    for dx, dy in COL_STEPS:
        greet(col_device(dx, (4 - dy) % 4))
    for dx, dz in ROW_STEPS:
        greet(row_device(dx, (4 - dz) % 4))
    for step in (1, 3):
        greet(x_device(4 - step))

    @pl.when(jnp.logical_not(own_self))
    def _():
        greet(own_from)
        pl.semaphore_wait(barrier, 18)

    @pl.when(own_self)
    def _():
        pl.semaphore_wait(barrier, 17)

    mine = y * 2 + core
    y_copies = []
    for i, dy in enumerate((1, 3, 2)):
        dev = y_device(dy)
        y_copies.append(
            (
                remote(pa_ref, xa.at[mine], y_send.at[0, i], y_recv.at[0, i], dev),
                remote(pb_ref, xb.at[mine], y_send.at[1, i], y_recv.at[1, i], dev),
            )
        )
    mate_copies = [
        (
            remote(pa_ref, xa.at[mine], c_send.at[0, 0], c_recv.at[0, 0], mate),
            remote(pb_ref, xb.at[mine], c_send.at[1, 0], c_recv.at[1, 0], mate),
        )
    ]
    for pair in mate_copies:
        for copy in pair:
            copy.start()
    for ab in range(2):
        for pair in y_copies:
            pair[ab].start()

    gpt = gpt_ref[...]
    table = jnp.concatenate([gpt >> 7, gpt & 127], axis=0).astype(F32).astype(BF16)
    own_start = r * (OWN * 16) + c * OWN
    tile = 1024

    def place(t, hits):
        ch = chosen_ref[:, pl.ds(pl.multiple_of(t * tile, tile), tile)]
        pick = jnp.where(
            lax.broadcasted_iota(jnp.int32, (96, tile), 0) == (ch >> 7), 1.0, 0.0
        ).astype(BF16)
        found = dot_nn(table, pick)
        value = found[:128] * 128.0 + found[128:]
        value = jnp.where(
            lax.broadcasted_iota(jnp.int32, (128, tile), 0) == (ch & 127), value, 0.0
        )
        position = jnp.sum(value, axis=0, keepdims=True).astype(jnp.int32)
        gb[:, pl.ds(pl.multiple_of(t * tile, tile), tile)] = position
        same = lax.broadcasted_iota(jnp.int32, (OWN, tile), 0) + own_start == position
        same = jnp.where(same, 1.0, 0.0)
        for i in range(tile // 128):
            hits = hits + same[:, i * 128 : (i + 1) * 128]
        return hits

    hits = lax.fori_loop(0, 8192 // tile, place, jnp.zeros((OWN, 128), F32))
    out_sel_ref[...] = jnp.broadcast_to(jnp.sum(hits, axis=1, keepdims=True), (OWN, 128))

    block_copy.wait()

    def divide(i, carry):
        rows = b_f32[pl.ds(pl.multiple_of(i * OWN, OWN), OWN), :]
        high, low = split(rows)
        b_high[i % 2, pl.ds(pl.multiple_of((i // 2) * OWN, OWN), OWN), :] = high
        b_low[i % 2, pl.ds(pl.multiple_of((i // 2) * OWN, OWN), OWN), :] = low
        return carry

    lax.fori_loop(0, 16, divide, 0)

    def take(panel, positions, first):
        width = panel.shape[1]
        hit = lax.broadcasted_iota(jnp.int32, (MA, width), 0) + first == positions
        hot = jnp.where(hit, 1.0, 0.0).astype(BF16)
        high, low = split(panel)
        both = dot_nt(jnp.concatenate([high, low], axis=0), hot)
        return both[:FEAT] + both[FEAT:]

    def gather(slot, target, to_x):
        first = ((to_x * 4 + y) * 2 + core) * MA
        source = x_hi * 8 + slot
        pos_a = gp_ref[:, pl.ds(pl.multiple_of(source * MA, 128), MA)]
        pos_b = gb[:, pl.ds(pl.multiple_of(source * MB, 128), MB)]
        target[:FEAT, :] += take(xa[slot], pos_a, first)
        target[FEAT:, :] += take(xb[slot], pos_b, first)

    xa[mine] = pa_ref[...]
    xb[mine] = pb_ref[...]
    near[...] = jnp.zeros_like(near)
    far[...] = jnp.zeros_like(far)
    gather(mine, far, 1 - x_hi)
    for copy in mate_copies[0]:
        copy.wait()
    gather(y * 2 + 1 - core, far, 1 - x_hi)
    for i, dy in enumerate((1, 3, 2)):
        from_slot = ((y + 4 - dy) % 4) * 2 + core
        pair = []
        for ab, buf in enumerate((xa, xb)):
            y_copies[i][ab].wait_recv()
            copy = remote(
                buf.at[from_slot],
                buf.at[from_slot],
                c_send.at[ab, i + 1],
                c_recv.at[ab, i + 1],
                mate,
            )
            copy.start()
            pair.append(copy)
        mate_copies.append(pair)
        gather(from_slot, far, 1 - x_hi)
        for copy in pair:
            copy.wait_recv()
        gather(((y + 4 - dy) % 4) * 2 + 1 - core, far, 1 - x_hi)
    far_copy = remote(far, far_in, far_send, far_recv, col_device(1, 0))
    far_copy.start()

    def gather_near(i, carry):
        gather(i, near, x_hi)
        return carry

    lax.fori_loop(0, 8, gather_near, 0)
    far_copy.wait()
    near[...] += far_in[...]
    for i in range(3):
        for ab in range(2):
            y_copies[i][ab].wait_send()
            mate_copies[i + 1][ab].wait_send()

    row_copies = []
    for ab in range(2):
        mine_f = near.at[pl.ds(ab * FEAT, FEAT), :]
        for i, (dx, dz) in enumerate(ROW_STEPS):
            copy = remote(
                mine_f,
                full.at[ab, r],
                row_send.at[ab, i],
                row_recv.at[ab, i],
                row_device(dx, dz),
            )
            copy.start()
            row_copies.append(copy)

    def store_full(ab, slot, value):
        high, low = split(value)
        full_high[ab, pl.ds(pl.multiple_of(slot * FEAT, FEAT), FEAT), :] = high
        full_low[ab, pl.ds(pl.multiple_of(slot * FEAT, FEAT), FEAT), :] = low

    for ab in range(2):
        store_full(ab, r, near[ab * FEAT : (ab + 1) * FEAT, :])

    def multiply(ab, part, target):
        def step(i, carry):
            rows = pl.ds(pl.multiple_of(i * 384, 384), 384)
            bh = b_high[part, rows, :]
            bl = b_low[part, rows, :]
            fh = full_high[ab]
            fl = full_low[ab]
            target[ab, rows, :] = dot_nt(bh, fh) + (dot_nt(bh, fl) + dot_nt(bl, fh))
            return carry

        lax.fori_loop(0, 2, step, 0)

    half_copies = []
    ring_copies = []
    for ab in range(2):
        for i, (dx, dz) in enumerate(ROW_STEPS):
            row_copies[ab * 7 + i].wait_recv()
            slot = ((x_lo + dx) % 2) * 4 + (z + 4 - dz) % 4
            store_full(ab, slot, full[ab, slot])
        multiply(ab, 1 - core, half_out)
        copy = remote(half_out.at[ab], half_in.at[ab], half_send.at[ab], half_recv.at[ab], mate)
        copy.start()
        half_copies.append(copy)
        multiply(ab, core, half_own)
        copy.wait_recv()
        half_own[ab] += half_in[ab]
        for i, (dx, dy) in enumerate(COL_STEPS):
            there = ((x_hi + dx) % 2) * 4 + (y + dy) % 4
            copy = remote(
                half_own.at[ab, pl.ds(pl.multiple_of(there * OWN, OWN), OWN), :],
                ring_in.at[ab, i],
                ring_send.at[ab, i],
                ring_recv.at[ab, i],
                col_device(dx, dy),
            )
            copy.start()
            ring_copies.append(copy)
    for copy in row_copies:
        copy.wait_send()

    pick = jnp.where(
        jnp.logical_and(
            lax.broadcasted_iota(jnp.int32, (128, MA), 0) + r * OWN
            == lax.broadcasted_iota(jnp.int32, (128, MA), 1),
            lax.broadcasted_iota(jnp.int32, (128, MA), 0) < OWN,
        ),
        1.0,
        0.0,
    ).astype(BF16)
    for ab in range(2):
        own_out[pl.ds(ab * W, W), :] = dot_nt(full_high[ab], pick) + dot_nt(full_low[ab], pick)
    own_copy = remote(own_out, own_in, own_send, own_recv, own_to)

    @pl.when(jnp.logical_not(own_self))
    def _():
        own_copy.start()

    @pl.when(own_self)
    def _():
        own_in[...] = own_out[...]

    here = pl.ds(pl.multiple_of((x_hi * 4 + y) * OWN, OWN), OWN)
    outs = (out_pa_ref, out_pb_ref)
    for ab in range(2):
        half_copies[ab].wait_send()
        total = half_own[ab, here, :]
        for i in range(7):
            ring_copies[ab * 7 + i].wait_recv()
            total = total + ring_in[ab, i]
        outs[ab][...] = total
    for copy in ring_copies:
        copy.wait_send()

    @pl.when(jnp.logical_not(own_self))
    def _():
        own_copy.wait()

    pad = jnp.zeros((128 - OWN, W), F32)
    ph_a, pl_a = split(jnp.concatenate([out_pa_ref[...], pad], axis=0))
    ph_b, pl_b = split(jnp.concatenate([out_pb_ref[...], pad], axis=0))
    fh_a, fl_a = split(own_in[:W, :])
    fh_b, fl_b = split(own_in[W:, :])

    def gram_of(fh, fl, ph, plow):
        return dot_nn(fh, ph) + (dot_nn(fh, plow) + dot_nn(fl, ph))

    gram[0:W, :] = gram_of(fh_a, fl_a, ph_a, pl_a)
    gram[W : 2 * W, :] = gram_of(fh_a, fl_a, ph_b, pl_b)
    gram[2 * W : 3 * W, :] = gram_of(fh_b, fl_b, ph_b, pl_b)
    half = 3 * W // 2
    copy = remote(
        gram.at[pl.ds(pl.multiple_of((1 - core) * half, half), half), :],
        gram_core,
        gc_send.at[0],
        gc_recv.at[0],
        mate,
    )
    copy.start()
    copy.wait()
    gram_core[...] += gram[pl.ds(pl.multiple_of(core * half, half), half), :]

    dims = ((x, x_device), (y, y_device), (z, z_device))
    orders = ((0, 1, 2), (1, 2, 0), (2, 0, 1))
    levels = []
    for p, order in enumerate(orders):
        q = [dims[d][0] for d in order]
        levels.append(
            (
                pl.multiple_of(p * 256, 256),
                q,
                [dims[d][1] for d in order],
            )
        )
    copies = []
    for p, (base, q, dev) in enumerate(levels):
        for i, step in enumerate((1, 3, 2)):
            to = (q[0] + step) % 4
            copy = remote(
                gram_core.at[pl.ds(pl.multiple_of(base + to * 64, 64), 64), :],
                gram_1.at[p, i],
                gs_send.at[0, p, i],
                gs_recv.at[0, p, i],
                dev[0](step),
            )
            copy.start()
            copies.append(copy)
    for p, (base, q, dev) in enumerate(levels):
        rows = pl.ds(pl.multiple_of(base + q[0] * 64, 64), 64)
        for i in range(3):
            copies[p * 3 + i].wait()
        gram_core[rows, :] += gram_1[p, 0] + gram_1[p, 1] + gram_1[p, 2]
        for i, step in enumerate((1, 3, 2)):
            to = (q[1] + step) % 4
            copy = remote(
                gram_core.at[pl.ds(pl.multiple_of(base + q[0] * 64 + to * 16, 16), 16), :],
                gram_2.at[p, i],
                gs_send.at[1, p, i],
                gs_recv.at[1, p, i],
                dev[1](step),
            )
            copy.start()
            copies.append(copy)
    for p, (base, q, dev) in enumerate(levels):
        rows = pl.ds(pl.multiple_of(base + q[0] * 64 + q[1] * 16, 16), 16)
        for i in range(3):
            copies[9 + p * 3 + i].wait()
        gram_core[rows, :] += gram_2[p, 0] + gram_2[p, 1] + gram_2[p, 2]
        for i, step in enumerate((1, 3, 2)):
            to = (q[2] + step) % 4
            copy = remote(
                gram_core.at[rows, pl.ds(pl.multiple_of(to * 128, 128), 128)],
                gram_3.at[p, i],
                gs_send.at[2, p, i],
                gs_recv.at[2, p, i],
                dev[2](step),
            )
            copy.start()
            copies.append(copy)
    home = core * half
    back = []

    def spread(level, p, ref, device):
        for i, step in enumerate((1, 3, 2)):
            copy = remote(
                ref, ref, gg_send.at[level, p, i], gg_recv.at[level, p, i], device(step)
            )
            copy.start()
            back.append(copy)

    for p, (base, q, dev) in enumerate(levels):
        row = base + q[0] * 64 + q[1] * 16
        column = pl.ds(pl.multiple_of(q[2] * 128, 128), 128)
        for i in range(3):
            copies[18 + p * 3 + i].wait()
        out_g_ref[pl.ds(pl.multiple_of(home + row, 16), 16), column] = (
            gram_core[pl.ds(pl.multiple_of(row, 16), 16), column]
            + gram_3[p, 0]
            + gram_3[p, 1]
            + gram_3[p, 2]
        )
        spread(0, p, out_g_ref.at[pl.ds(pl.multiple_of(home + row, 16), 16), column], dev[2])
    for p, (base, q, dev) in enumerate(levels):
        for i in range(3):
            back[p * 3 + i].wait()
        row = home + base + q[0] * 64 + q[1] * 16
        spread(1, p, out_g_ref.at[pl.ds(pl.multiple_of(row, 16), 16), :], dev[1])
    for p, (base, q, dev) in enumerate(levels):
        for i in range(3):
            back[9 + p * 3 + i].wait()
        row = home + base + q[0] * 64
        spread(2, p, out_g_ref.at[pl.ds(pl.multiple_of(row, 64), 64), :], dev[0])
    last = []
    for p, (base, q, dev) in enumerate(levels):
        for i in range(3):
            back[18 + p * 3 + i].wait()
        part = out_g_ref.at[pl.ds(pl.multiple_of(home + base, 256), 256), :]
        copy = remote(part, part, gc_send.at[1 + p], gc_recv.at[1 + p], mate)
        copy.start()
        last.append(copy)
    for copy in last:
        copy.wait()


def final_kernel(
    pa_ref, pb_ref, sel_ref, g_ref, pivot_a_ref, top_ref, pivot_b_ref, ia_ref, da_ref, ib_ref, tb_ref, db_ref
):
    top = top_ref[...]
    product_a = pa_ref[...]
    ia_ref[...] = -product_a
    ib_ref[...] = -(pb_ref[...] - dot3(product_a, top)) * sel_ref[:, :1]
    diagonal_a = pivot_a_ref[...] + g_ref[:W, :]
    da_ref[...] = diagonal_a
    cross_neg = g_ref[W : 2 * W, :]
    top_b = cross_neg - dot3(diagonal_a, top)
    tb_ref[...] = top_b
    top_t = top.T
    db_ref[...] = (
        pivot_b_ref[...] - dot3(top_t, top_b) + (g_ref[2 * W :, :] - dot3(cross_neg.T, top))
    )


def body(
    inverse_block,
    grid_position,
    panel_a,
    pivot_inverse_a,
    chosen_rows,
    top_panel_b,
    panel_b,
    pivot_inverse_b,
):
    vmem = pl.BlockSpec(memory_space=pltpu.VMEM)
    dma = pltpu.SemaphoreType.DMA
    out = jax.ShapeDtypeStruct
    gp = grid_position.reshape(1, -1)
    gpt = grid_position.reshape(96, 128).T
    product_a, product_b, selected, gram = pl.pallas_call(
        main_kernel,
        out_shape=(
            out((OWN, W), F32),
            out((OWN, W), F32),
            out((OWN, 128), F32),
            out((3 * W, W), F32),
        ),
        in_specs=[pl.BlockSpec(memory_space=pl.ANY)] + [vmem] * 5,
        out_specs=(vmem,) * 4,
        scratch_shapes=[
            pltpu.VMEM((1536, MA), F32),
            pltpu.VMEM((2, 768, MA), BF16),
            pltpu.VMEM((2, 768, MA), BF16),
            pltpu.VMEM((1, 8192), jnp.int32),
            pltpu.VMEM((8, FEAT, MA), F32),
            pltpu.VMEM((8, FEAT, MB), F32),
            pltpu.VMEM((2 * FEAT, MA), F32),
            pltpu.VMEM((2 * FEAT, MA), F32),
            pltpu.VMEM((2 * FEAT, MA), F32),
            pltpu.VMEM((2, 8, FEAT, MA), F32),
            pltpu.VMEM((2, W, MA), BF16),
            pltpu.VMEM((2, W, MA), BF16),
            pltpu.VMEM((2, 768, W), F32),
            pltpu.VMEM((2, 768, W), F32),
            pltpu.VMEM((2, 768, W), F32),
            pltpu.VMEM((2, 7, OWN, W), F32),
            pltpu.VMEM((2 * W, 128), F32),
            pltpu.VMEM((2 * W, 128), F32),
            pltpu.VMEM((3 * W, W), F32),
            pltpu.VMEM((3 * W // 2, W), F32),
            pltpu.VMEM((3, 3, 64, W), F32),
            pltpu.VMEM((3, 3, 16, W), F32),
            pltpu.VMEM((3, 3, 16, 128), F32),
            dma,
            dma((2, 3)),
            dma((2, 3)),
            dma((2, 4)),
            dma((2, 4)),
            dma,
            dma,
            dma((2, 7)),
            dma((2, 7)),
            dma((2,)),
            dma((2,)),
            dma((2, 7)),
            dma((2, 7)),
            dma,
            dma,
            dma((4,)),
            dma((4,)),
            dma((3, 3, 3)),
            dma((3, 3, 3)),
            dma((3, 3, 3)),
            dma((3, 3, 3)),
        ],
        compiler_params=pltpu.CompilerParams(
            collective_id=0, has_side_effects=True, vmem_limit_bytes=60 << 20
        ),
        cost_estimate=pl.CostEstimate(
            flops=10_000_000_000, bytes_accessed=20_000_000, transcendentals=0
        ),
        name="exchange",
    )(inverse_block, gp, gpt, chosen_rows.reshape(1, -1), panel_a, panel_b)
    return pl.pallas_call(
        final_kernel,
        out_shape=(
            out((OWN, W), F32),
            out((W, W), F32),
            out((OWN, W), F32),
            out((W, W), F32),
            out((W, W), F32),
        ),
        in_specs=[vmem] * 7,
        out_specs=(vmem,) * 5,
        compiler_params=pltpu.CompilerParams(vmem_limit_bytes=48 << 20),
        name="finish",
    )(product_a, product_b, selected, gram, pivot_inverse_a, top_panel_b, pivot_inverse_b)


def solution(mesh):
    in_specs = (P("row", "col"), P(), P("row", "col"), P(), P(), P(), P("row", "col"), P())
    out_specs = (P(("row", "col"), None), P(), P(("row", "col"), None), P(), P())
    return jax.shard_map(body, mesh=mesh, in_specs=in_specs, out_specs=out_specs, check_vma=False)
```

time: 631 us -> 182 us (0.29)
  waiting for transfers between devices: 406 us -> 0 us
  Pallas kernels: 0 us -> 177 us
  local copies, waits for them, and re-layouts: 166 us -> 4.18 us
  matrix products: 37.4 us -> 0 us
  between operations: 14.2 us -> 0.68 us
  other arithmetic: 6.35 us -> 0 us
    pallas_call x0 -> x2, Pallas kernels: none -> 177 us  [the longest x1 171 us: body(): pl.pallas_call(main_kernel, out_shape=(out((OWN, W), F32), out((OWN, W),...]
    psum x1 -> x0, waiting for transfers between devices: 150 us -> none  [body(): diag_total, cross = lax.psum((diag_part, cross_part), ('row', 'col'))]
    all_gather x6 -> x0, waiting for transfers between devices: 108 us -> none  [the longest x1 39.1 us: body(): lax.all_gather(pick_columns(wide_b, group_b, count), 'row', axis=0, tiled...]
    reduce_scatter x1 -> x0, waiting for transfers between devices: 80.5 us -> none  [body(): lax.psum_scatter(project(inverse_block, cols_b), 'col', scatter_dimension...]
    scatter x2 -> x0, local copies, waits for them, and re-layouts: 75.9 us -> none  [the longest x1 45.4 us: body(): jnp.zeros((order,), jnp.int32).at[grid_position]]
    gather x11 -> x0, local copies, waits for them, and re-layouts: 71.3 us -> none  [the longest x1 45.5 us: body(): grid_position[chosen_rows]]
    unnamed x10 -> x0, waiting for transfers between devices: 68.6 us -> none
    dot_general x8 -> x0, matrix products: 37.4 us -> none  [the longest x2 22.6 us: project(): lax.dot_general(block, panel_t, (((1,), (1,)), ((), ())), precision=lax.P...]
  transfers between devices with their start and end apart: 9 -> 0, of which waited for: 8 -> 0; matrix products, arithmetic and copies ran while one was open for 31% -> 0% of each run, Pallas kernels for 0% -> 0%
where the time goes in v1:
time: 182 us
  Pallas kernels  177 us (97%)
  local copies, waits for them, and re-layouts  4.18 us (2%)
    pallas_call x1, Pallas kernels, body(): pl.pallas_call(main_kernel, out_shape=(out((OWN, W), F32), out((OWN, W),...  171 us
    pallas_call x1, Pallas kernels, body(): pl.pallas_call(final_kernel, out_shape=(out((OWN, W), F32), out((W, W), F...  5.89 us

profile of v1, /device:TPU:1, one launch (start us, length us, event | category | flops | bytes accessed | tf_op | source)
XLA Modules:
  0.0 182.1 jit_solution(13704704084473271825)
XLA Ops:
  0.6 1.5 copy.13
  2.2 0.0 copy-start
  2.2 0.0 copy-start.1
  2.2 0.0 copy-start.2
  2.2 171.3 %exchange.1 = (f32[96,512]{1,0:T(8,128)}, f32[96,512]{1,0:T(8,128)}, f32[96,128]{1,0:T(8,128)}, f32[1536,512]{1,0:T(8,128)}) custom-call(f32[1536,768]{1,0:T(8,128)} %block_ref.1, s32[1,12288]{1,0:T(1,128)} %bitcast.6, s32[128,96]{1,0:T(8,128)} %bitcast.4, s32[1,8192]{1,0:T(1,128)} %bitcast.7, f32[64,768]{1,0:T(8,128)} %pa_ref.1, f32[64,512]{1,0:T(8,128)} %pb_ref.1), custom_call_target="tpu_custom_call" | custom-call | flops 10000000000 | bytes 20000000 | tf_op jit(solution)/shard_map/exchange/pallas_call | solution.py:537
  173.5 0.0 copy-done
  173.5 0.0 copy-done.1
  173.5 0.0 copy-done.2
  173.5 0.0 copy-start.3
  173.5 0.9 copy-done.3
  174.5 0.0 copy-start.4
  174.5 0.9 copy-done.4
  175.4 0.0 copy-start.5
  175.4 0.8 copy-done.5
  176.2 5.9 %finish.1 = (f32[96,512]{1,0:T(8,128)}, f32[512,512]{1,0:T(8,128)}, f32[96,512]{1,0:T(8,128)}, f32[512,512]{1,0:T(8,128)}, f32[512,512]{1,0:T(8,128)}) custom-call(f32[96,512]{1,0:T(8,128)S(1)} %copy-done.3, f32[96,512]{1,0:T(8,128)S(1)} %copy-done.4, f32[96,128]{1,0:T(8,128)S(1)} %copy-done.5, f32[1536,512]{1,0:T(8,128)} %get-tuple-element.12.g_ref, ...), custom_call_target="tpu_custom_call" | custom-call | tf_op jit(solution)/shard_map/finish/pallas_call | solution.py:601
Async XLA Ops:
  2.2 171.3 %copy-start = (f32[512,512]{1,0:T(8,128)S(1)}, f32[512,512]{1,0:T(8,128)}, u32[]{:S(2)}) copy-start(f32[512,512]{1,0:T(8,128)} %pivot_a_ref.1) | copy-start | bytes 3145732
  2.2 171.4 %copy-start.1 = (f32[512,512]{1,0:T(8,128)S(1)}, f32[512,512]{1,0:T(8,128)}, u32[]{:S(2)}) copy-start(f32[512,512]{1,0:T(8,128)} %top_ref.1) | copy-start | bytes 3145732
  2.2 171.4 %copy-start.2 = (f32[512,512]{1,0:T(8,128)S(1)}, f32[512,512]{1,0:T(8,128)}, u32[]{:S(2)}) copy-start(f32[512,512]{1,0:T(8,128)} %pivot_b_ref.1) | copy-start | bytes 3145732
  173.5 0.9 copy-start.3
  174.5 0.9 copy-start.4
  175.4 0.8 copy-start.5

commit v2 on v1

v2 whole, which is shorter than its diff:
```python
import functools

import jax
import jax.numpy as jnp
from jax import lax
from jax.experimental import pallas as pl
from jax.experimental.pallas import tpu as pltpu
from jax.sharding import PartitionSpec as P

MESH = pl.DeviceIdType.MESH
F32 = jnp.float32
BF16 = jnp.bfloat16
NT = (((1,), (1,)), ((), ()))
W = 512
FEAT = 64
MA = 768
MB = 512
OWN = 96


def split(x):
    high = x.astype(BF16)
    return high, (x - high.astype(F32)).astype(BF16)


def dot_nn(a, b):
    return jnp.dot(a, b, preferred_element_type=F32)


def dot_nt(a, b):
    return lax.dot_general(a, b, NT, preferred_element_type=F32)


def dot3(a, b):
    ah, al = split(a)
    bh, bl = split(b)
    return dot_nn(ah, bh) + (dot_nn(ah, bl) + dot_nn(al, bh))


def remote(src, dst, send, recv, device):
    return pltpu.make_async_remote_copy(
        src_ref=src,
        dst_ref=dst,
        send_sem=send,
        recv_sem=recv,
        device_id=device,
        device_id_type=MESH,
    )


def main_kernel(
    block_ref,
    gp_ref,
    gpt_ref,
    chosen_ref,
    pa_ref,
    pb_ref,
    out_pa_ref,
    out_pb_ref,
    out_sel_ref,
    out_g_ref,
    b_f32,
    b_high,
    b_low,
    gb,
    xa,
    xb,
    near,
    far,
    far_in,
    full,
    full_high,
    full_low,
    half_out,
    half_in,
    half_own,
    ring_2,
    ring_1,
    x_out,
    x_in,
    own_out,
    own_in,
    gram,
    gram_core,
    gram_1,
    gram_2,
    gram_3,
    b_sem,
    y_send,
    y_recv,
    c_send,
    c_recv,
    far_send,
    far_recv,
    row_send,
    row_recv,
    half_send,
    half_recv,
    ring_send,
    ring_recv,
    x_send,
    x_recv,
    own_send,
    own_recv,
    gc_send,
    gc_recv,
    gs_send,
    gs_recv,
    gg_send,
    gg_recv,
):
    r = lax.axis_index("row")
    c = lax.axis_index("col")
    x_lo, z = r // 4, r % 4
    x_hi, y, core = c // 8, (c // 2) % 4, c % 2
    x = x_hi * 2 + x_lo
    mate = (r, c + 1 - 2 * core)

    def x_device(dx):
        nx = (x + dx) % 4
        return ((nx % 2) * 4 + z, ((nx // 2) * 4 + y) * 2 + core)

    def y_device(dy):
        return (r, (x_hi * 4 + (y + dy) % 4) * 2 + core)

    def z_device(dz):
        return (x_lo * 4 + (z + dz) % 4, c)

    x_pair = ((1 - x_lo) * 4 + z, c)
    x_across = x_device(2)
    own_to = (c // 2, (c % 2) * 8 + r)
    own_from = (c % 8, 2 * r + c // 8)
    own_self = jnp.logical_and(own_to[0] == r, own_to[1] == c)
    pending = []

    def send(src, dst, send_sem, recv_sem, device):
        copy = remote(src, dst, send_sem, recv_sem, device)
        copy.start()
        pending.append(copy)
        return copy

    def rows_of(start, size):
        return pl.ds(pl.multiple_of(start, size), size)

    block_copy = pltpu.make_async_copy(block_ref, b_f32, b_sem)
    block_copy.start()

    barrier = pltpu.get_barrier_semaphore()

    def greet(device):
        pl.semaphore_signal(barrier, inc=1, device_id=device, device_id_type=MESH)

    greet(mate)
    for step in (1, 2, 3):
        greet(x_device(4 - step))
        greet(y_device(4 - step))
        greet(z_device(4 - step))

    @pl.when(jnp.logical_not(own_self))
    def _():
        greet(own_from)
        pl.semaphore_wait(barrier, 11)

    @pl.when(own_self)
    def _():
        pl.semaphore_wait(barrier, 10)

    mine = y * 2 + core
    steps = (1, 3, 2)
    panels = (pa_ref, pb_ref)
    held = (xa, xb)
    y_copies = []
    mate_copies = []
    for ab in range(2):
        mate_copies.append(
            [send(panels[ab], held[ab].at[mine], c_send.at[ab, 0], c_recv.at[ab, 0], mate)]
        )
        y_copies.append(
            [
                send(
                    panels[ab], held[ab].at[mine], y_send.at[ab, i], y_recv.at[ab, i], y_device(dy)
                )
                for i, dy in enumerate(steps)
            ]
        )

    def pass_on(ab, i):
        slot = ((y + 4 - steps[i]) % 4) * 2 + core
        y_copies[ab][i].wait_recv()
        ref = held[ab].at[slot]
        mate_copies[ab].append(send(ref, ref, c_send.at[ab, i + 1], c_recv.at[ab, i + 1], mate))

    block_copy.wait()

    def divide(i, carry):
        high, low = split(b_f32[rows_of(i * OWN, OWN), :])
        b_high[i % 2, rows_of((i // 2) * OWN, OWN), :] = high
        b_low[i % 2, rows_of((i // 2) * OWN, OWN), :] = low
        return carry

    lax.fori_loop(0, 16, divide, 0)

    gpt = gpt_ref[...]
    table = jnp.concatenate([gpt >> 7, gpt & 127], axis=0).astype(F32).astype(BF16)
    own_start = r * (OWN * 16) + c * OWN
    tile = 1024

    def place(t, hits):
        ch = chosen_ref[:, rows_of(t * tile, tile)]
        pick = jnp.where(
            lax.broadcasted_iota(jnp.int32, (96, tile), 0) == (ch >> 7), 1.0, 0.0
        ).astype(BF16)
        found = dot_nn(table, pick)
        value = found[:128] * 128.0 + found[128:]
        value = jnp.where(
            lax.broadcasted_iota(jnp.int32, (128, tile), 0) == (ch & 127), value, 0.0
        )
        position = jnp.sum(value, axis=0, keepdims=True).astype(jnp.int32)
        gb[:, rows_of(t * tile, tile)] = position
        same = lax.broadcasted_iota(jnp.int32, (OWN, tile), 0) + own_start == position
        same = jnp.where(same, 1.0, 0.0)
        for i in range(tile // 128):
            hits = hits + same[:, i * 128 : (i + 1) * 128]
        return hits

    def take(panel, positions, first):
        width = panel.shape[1]
        hit = lax.broadcasted_iota(jnp.int32, (MA, width), 0) + first == positions
        hot = jnp.where(hit, 1.0, 0.0).astype(BF16)
        high, low = split(panel)
        both = dot_nt(jnp.concatenate([high, low], axis=0), hot)
        return both[:FEAT] + both[FEAT:]

    def gather(ab, slot, target, to_x):
        first = ((to_x * 4 + y) * 2 + core) * MA
        source = x_hi * 8 + slot
        if ab == 0:
            positions = gp_ref[:, pl.ds(pl.multiple_of(source * MA, 128), MA)]
        else:
            positions = gb[:, pl.ds(pl.multiple_of(source * MB, 128), MB)]
        target[ab] += take(held[ab][slot], positions, first)

    xa[mine] = pa_ref[...]
    xb[mine] = pb_ref[...]
    near[...] = jnp.zeros_like(near)
    far[...] = jnp.zeros_like(far)

    def gather_far(ab):
        gather(ab, mine, far, 1 - x_hi)
        mate_copies[ab][0].wait_recv()
        gather(ab, y * 2 + 1 - core, far, 1 - x_hi)
        for i, dy in enumerate(steps):
            base = ((y + 4 - dy) % 4) * 2
            if ab == 0:
                pass_on(ab, i)
            gather(ab, base + core, far, 1 - x_hi)
            mate_copies[ab][i + 1].wait_recv()
            gather(ab, base + 1 - core, far, 1 - x_hi)
        return send(far.at[ab], far_in.at[ab], far_send.at[ab], far_recv.at[ab], x_across)

    def gather_near(ab):
        def step(i, carry):
            gather(ab, i, near, x_hi)
            return carry

        lax.fori_loop(0, 8, step, 0)

    def store_full(ab, slot, value):
        high, low = split(value)
        full_high[ab, rows_of(slot * FEAT, FEAT), :] = high
        full_low[ab, rows_of(slot * FEAT, FEAT), :] = low

    row_copies = [{}, {}]
    sets = (x_lo, 1 - x_lo)

    def row_put(ab, name, src, slot, part, k, device):
        dst = full.at[ab, slot]
        if part is not None:
            dst = dst.at[pl.ds(part * 32, 32), :]
        row_copies[ab][name] = send(
            dst if src is None else src, dst, row_send.at[ab, k], row_recv.at[ab, k], device
        )

    def row_start(ab):
        src = near.at[ab]
        row_put(ab, "pair", src, r, None, 0, x_pair)
        row_put(ab, "up0", src, r, None, 1, z_device(1))
        row_put(ab, "down0", src, r, None, 2, z_device(3))
        store_full(ab, r, near[ab])

    def row_turn(ab, s):
        base = sets[s] * 4
        below = base + (z + 3) % 4
        above = base + (z + 1) % 4
        row_copies[ab]["up%d" % s].wait_recv()
        row_put(ab, "far_up%d" % s, None, below, 0, 3 + 4 * s, z_device(1))
        row_copies[ab]["down%d" % s].wait_recv()
        row_put(ab, "far_down%d" % s, None, above, 1, 4 + 4 * s, z_device(3))
        if s == 0:
            other = (1 - x_lo) * 4 + z
            row_copies[ab]["pair"].wait_recv()
            row_put(ab, "up1", None, other, None, 5, z_device(1))
            row_put(ab, "down1", None, other, None, 6, z_device(3))
            store_full(ab, other, full[ab, other])
        store_full(ab, below, full[ab, below])
        store_full(ab, above, full[ab, above])

    def row_end(ab):
        for s in range(2):
            slot = sets[s] * 4 + (z + 2) % 4
            row_copies[ab]["far_up%d" % s].wait_recv()
            row_copies[ab]["far_down%d" % s].wait_recv()
            store_full(ab, slot, full[ab, slot])

    halves = (1 - x_hi, x_hi)

    def multiply(ab, part, half, target):
        rows = rows_of(half * 384, 384)
        bh = b_high[part, rows, :]
        bl = b_low[part, rows, :]
        fh = full_high[ab]
        fl = full_low[ab]
        target[ab, rows, :] = dot_nt(bh, fh) + (dot_nt(bh, fl) + dot_nt(bl, fh))

    half_copies = [[None, None], [None, None]]

    def product_out(ab, s):
        rows = rows_of(halves[s] * 384, 384)
        multiply(ab, 1 - core, halves[s], half_out)
        half_copies[ab][s] = send(
            half_out.at[ab, rows, :],
            half_in.at[ab, rows, :],
            half_send.at[ab, s],
            half_recv.at[ab, s],
            mate,
        )

    def product_own(ab, s):
        rows = rows_of(halves[s] * 384, 384)
        multiply(ab, core, halves[s], half_own)
        half_copies[ab][s].wait_recv()
        half_own[ab, rows, :] += half_in[ab, rows, :]

    ring_copies = {}

    def chunk(s, dy, part=None):
        start = (halves[s] * 4 + (y + dy) % 4) * OWN
        if part is None:
            return rows_of(start, OWN)
        return rows_of(start + part * 48, 48)

    def ring_put(ab, s, name, k, src_rows, dst, device):
        ring_copies[ab, s, name] = send(
            half_own.at[ab, src_rows, :], dst, ring_send.at[ab, s, k], ring_recv.at[ab, s, k], device
        )

    low_part = pl.ds(0, 48)
    high_part = pl.ds(48, 48)

    def ring_start(ab, s):
        up, down = y_device(1), y_device(3)
        ring_put(ab, s, "two_up", 0, chunk(s, 2, 0), ring_2.at[ab, s, 0], up)
        ring_put(ab, s, "two_down", 1, chunk(s, 2, 1), ring_2.at[ab, s, 1], down)
        ring_put(ab, s, "up_high", 2, chunk(s, 1, 1), ring_1.at[ab, s, 0, high_part, :], up)
        ring_put(ab, s, "down_low", 3, chunk(s, 3, 0), ring_1.at[ab, s, 1, low_part, :], down)

    def ring_turn(ab, s):
        up, down = y_device(1), y_device(3)
        ring_copies[ab, s, "two_up"].wait_recv()
        half_own[ab, chunk(s, 1, 0), :] += ring_2[ab, s, 0]
        ring_put(ab, s, "up_low", 4, chunk(s, 1, 0), ring_1.at[ab, s, 0, low_part, :], up)
        ring_copies[ab, s, "two_down"].wait_recv()
        half_own[ab, chunk(s, 3, 1), :] += ring_2[ab, s, 1]
        ring_put(ab, s, "down_high", 5, chunk(s, 3, 1), ring_1.at[ab, s, 1, high_part, :], down)

    def ring_sum(ab, s):
        for name in ("up_high", "down_low", "up_low", "down_high"):
            ring_copies[ab, s, name].wait_recv()
        return half_own[ab, chunk(s, 0), :] + ring_1[ab, s, 0] + ring_1[ab, s, 1]

    def ring_across(ab):
        x_out[ab] = ring_sum(ab, 0)
        ring_copies[ab] = send(
            x_out.at[ab], x_in.at[ab], x_send.at[ab], x_recv.at[ab], x_across
        )

    def ring_end(ab):
        total = ring_sum(ab, 1)
        ring_copies[ab].wait_recv()
        total = total + x_in[ab]
        (out_pa_ref, out_pb_ref)[ab][...] = total
        return total

    own_copies = []

    def own_start_copy(ab):
        line = lax.broadcasted_iota(jnp.int32, (128, MA), 0)
        pick = jnp.where(
            jnp.logical_and(
                line + r * OWN == lax.broadcasted_iota(jnp.int32, (128, MA), 1), line < OWN
            ),
            1.0,
            0.0,
        ).astype(BF16)
        own_out[ab] = dot_nt(full_high[ab], pick) + dot_nt(full_low[ab], pick)
        copy = remote(own_out.at[ab], own_in.at[ab], own_send.at[ab], own_recv.at[ab], own_to)
        own_copies.append(copy)

        @pl.when(jnp.logical_not(own_self))
        def _():
            copy.start()

        @pl.when(own_self)
        def _():
            own_in[ab] = own_out[ab]

    def own_wait(ab):
        @pl.when(jnp.logical_not(own_self))
        def _():
            own_copies[ab].wait()

    dims = ((x, x_device), (y, y_device), (z, z_device))
    parts = []
    for where, size, home, order in (
        (0, 256, core * 512, (0, 1, 2)),
        (256, 256, core * 512 + 256, (1, 2, 0)),
        (512, 128, 1024 + core * 256, (2, 0, 1)),
        (640, 128, 1024 + core * 256 + 128, (1, 2, 0)),
    ):
        q = [dims[d][0] for d in order]
        parts.append((where, size, home, q, [dims[d][1] for d in order]))
    gram_copies = {}

    def gram_step(p, n):
        where, size, home, q, dev = parts[p]
        one, two = size // 4, size // 16
        row_1 = q[0] * one
        row_2 = row_1 + q[1] * two
        column = pl.ds(pl.multiple_of(q[2] * 128, 128), 128)
        if n > 0:
            for copy in gram_copies[p, n - 1]:
                copy.wait_recv()
        copies = []
        gram_copies[p, n] = copies
        if n == 0:
            pass
        elif n == 1:
            rows = rows_of(where + row_1, one)
            got = [gram_1[p, i, 0:one, :] for i in range(3)]
            gram_core[rows, :] += got[0] + got[1] + got[2]
        elif n == 2:
            rows = rows_of(where + row_2, two)
            got = [gram_2[p, i, 0:two, :] for i in range(3)]
            gram_core[rows, :] += got[0] + got[1] + got[2]
        elif n == 3:
            rows = rows_of(where + row_2, two)
            got = [gram_3[p, i, 0:two, :] for i in range(3)]
            out_g_ref[rows_of(home + row_2, two), column] = (
                gram_core[rows, column] + got[0] + got[1] + got[2]
            )
        for i, step in enumerate(steps):
            if n == 0:
                src = gram_core.at[rows_of(where + ((q[0] + step) % 4) * one, one), :]
                dst = gram_1.at[p, i, pl.ds(0, one), :]
            elif n == 1:
                src = gram_core.at[rows_of(where + row_1 + ((q[1] + step) % 4) * two, two), :]
                dst = gram_2.at[p, i, pl.ds(0, two), :]
            elif n == 2:
                to = pl.ds(pl.multiple_of(((q[2] + step) % 4) * 128, 128), 128)
                src = gram_core.at[rows_of(where + row_2, two), to]
                dst = gram_3.at[p, i, pl.ds(0, two), :]
            elif n == 3:
                src = dst = out_g_ref.at[rows_of(home + row_2, two), column]
            elif n == 4:
                src = dst = out_g_ref.at[rows_of(home + row_2, two), :]
            elif n == 5:
                src = dst = out_g_ref.at[rows_of(home + row_1, one), :]
            if n < 6:
                d = dev[n if n < 3 else 5 - n]
                copies.append(send(src, dst, gs_send.at[p, n, i], gs_recv.at[p, n, i], d(step)))
        if n == 6:
            src = dst = out_g_ref.at[rows_of(home, size), :]
            copies.append(send(src, dst, gg_send.at[p], gg_recv.at[p], mate))

    def gram_of(f, p):
        fh, fl = split(f)
        ph, low = split(jnp.concatenate([p, jnp.zeros((128 - OWN, W), F32)], axis=0))
        return dot_nn(fh, ph) + (dot_nn(fh, low) + dot_nn(fl, ph))

    hits = lax.fori_loop(0, 8192 // tile, place, jnp.zeros((OWN, 128), F32))
    out_sel_ref[...] = jnp.broadcast_to(jnp.sum(hits, axis=1, keepdims=True), (OWN, 128))
    far_a = gather_far(0)
    gather_near(0)
    for i in range(3):
        pass_on(1, i)
    far_a.wait_recv()
    near[0] += far_in[0]
    row_start(0)
    far_b = gather_far(1)
    row_turn(0, 0)
    gather_near(1)
    far_b.wait_recv()
    near[1] += far_in[1]
    row_start(1)
    row_turn(0, 1)
    row_turn(1, 0)
    row_end(0)
    product_out(0, 0)
    product_out(0, 1)
    product_own(0, 0)
    ring_start(0, 0)
    product_own(0, 1)
    ring_start(0, 1)
    row_turn(1, 1)
    own_start_copy(0)
    ring_turn(0, 0)
    ring_turn(0, 1)
    row_end(1)
    product_out(1, 0)
    product_out(1, 1)
    ring_across(0)
    product_own(1, 0)
    ring_start(1, 0)
    product_own(1, 1)
    ring_start(1, 1)
    own_start_copy(1)
    product_a = ring_end(0)
    ring_turn(1, 0)
    ring_turn(1, 1)
    own_wait(0)
    gram[0:W, :] = gram_of(own_in[0], product_a)
    own_wait(1)
    gram[W : 2 * W, :] = gram_of(own_in[1], product_a)
    core_a = send(
        gram.at[rows_of((1 - core) * W, W), :],
        gram_core.at[0:W, :],
        gc_send.at[0],
        gc_recv.at[0],
        mate,
    )
    core_a.wait_recv()
    gram_core[0:W, :] += gram[rows_of(core * W, W), :]
    gram_step(0, 0)
    gram_step(1, 0)
    ring_across(1)
    gram_step(0, 1)
    gram_step(1, 1)
    product_b = ring_end(1)
    gram[2 * W : 3 * W, :] = gram_of(own_in[1], product_b)
    core_b = send(
        gram.at[rows_of(2 * W + (1 - core) * 256, 256), :],
        gram_core.at[W : W + 256, :],
        gc_send.at[1],
        gc_recv.at[1],
        mate,
    )
    gram_step(0, 2)
    gram_step(1, 2)
    core_b.wait_recv()
    gram_core[W : W + 256, :] += gram[rows_of(2 * W + core * 256, 256), :]
    gram_step(2, 0)
    gram_step(3, 0)
    gram_step(0, 3)
    gram_step(1, 3)
    for n in range(1, 7):
        gram_step(2, n)
        gram_step(3, n)
        if n + 3 < 7:
            gram_step(0, n + 3)
            gram_step(1, n + 3)
    for p in range(4):
        gram_copies[p, 6][0].wait_recv()
    for copy in pending:
        copy.wait_send()


def final_kernel(
    pa_ref, pb_ref, sel_ref, g_ref, pivot_a_ref, top_ref, pivot_b_ref, ia_ref, da_ref, ib_ref, tb_ref, db_ref
):
    top = top_ref[...]
    product_a = pa_ref[...]
    ia_ref[...] = -product_a
    ib_ref[...] = -(pb_ref[...] - dot3(product_a, top)) * sel_ref[:, :1]
    diagonal_a = pivot_a_ref[...] + g_ref[:W, :]
    da_ref[...] = diagonal_a
    cross_neg_t = g_ref[W : 2 * W, :]
    cross_neg = cross_neg_t.T
    top_b = cross_neg - dot3(diagonal_a, top)
    tb_ref[...] = top_b
    top_t = top.T
    db_ref[...] = (
        pivot_b_ref[...] - dot3(top_t, top_b) + (g_ref[2 * W :, :] - dot3(cross_neg_t, top))
    )


def body(
    inverse_block,
    grid_position,
    panel_a,
    pivot_inverse_a,
    chosen_rows,
    top_panel_b,
    panel_b,
    pivot_inverse_b,
):
    vmem = pl.BlockSpec(memory_space=pltpu.VMEM)
    dma = pltpu.SemaphoreType.DMA
    out = jax.ShapeDtypeStruct
    gp = grid_position.reshape(1, -1)
    gpt = grid_position.reshape(96, 128).T
    product_a, product_b, selected, gram = pl.pallas_call(
        main_kernel,
        out_shape=(
            out((OWN, W), F32),
            out((OWN, W), F32),
            out((OWN, 128), F32),
            out((3 * W, W), F32),
        ),
        in_specs=[pl.BlockSpec(memory_space=pl.ANY)] + [vmem] * 5,
        out_specs=(vmem,) * 4,
        scratch_shapes=[
            pltpu.VMEM((1536, MA), F32),
            pltpu.VMEM((2, 768, MA), BF16),
            pltpu.VMEM((2, 768, MA), BF16),
            pltpu.VMEM((1, 8192), jnp.int32),
            pltpu.VMEM((8, FEAT, MA), F32),
            pltpu.VMEM((8, FEAT, MB), F32),
            pltpu.VMEM((2, FEAT, MA), F32),
            pltpu.VMEM((2, FEAT, MA), F32),
            pltpu.VMEM((2, FEAT, MA), F32),
            pltpu.VMEM((2, 8, FEAT, MA), F32),
            pltpu.VMEM((2, W, MA), BF16),
            pltpu.VMEM((2, W, MA), BF16),
            pltpu.VMEM((2, 768, W), F32),
            pltpu.VMEM((2, 768, W), F32),
            pltpu.VMEM((2, 768, W), F32),
            pltpu.VMEM((2, 2, 2, 48, W), F32),
            pltpu.VMEM((2, 2, 2, OWN, W), F32),
            pltpu.VMEM((2, OWN, W), F32),
            pltpu.VMEM((2, OWN, W), F32),
            pltpu.VMEM((2, W, 128), F32),
            pltpu.VMEM((2, W, 128), F32),
            pltpu.VMEM((3 * W, W), F32),
            pltpu.VMEM((3 * W // 2, W), F32),
            pltpu.VMEM((4, 3, 64, W), F32),
            pltpu.VMEM((4, 3, 16, W), F32),
            pltpu.VMEM((4, 3, 16, 128), F32),
            dma,
            dma((2, 3)),
            dma((2, 3)),
            dma((2, 4)),
            dma((2, 4)),
            dma((2,)),
            dma((2,)),
            dma((2, 9)),
            dma((2, 9)),
            dma((2, 2)),
            dma((2, 2)),
            dma((2, 2, 6)),
            dma((2, 2, 6)),
            dma((2,)),
            dma((2,)),
            dma((2,)),
            dma((2,)),
            dma((2,)),
            dma((2,)),
            dma((4, 6, 3)),
            dma((4, 6, 3)),
            dma((4,)),
            dma((4,)),
        ],
        compiler_params=pltpu.CompilerParams(
            collective_id=0, has_side_effects=True, vmem_limit_bytes=60 << 20
        ),
        cost_estimate=pl.CostEstimate(
            flops=10_000_000_000, bytes_accessed=20_000_000, transcendentals=0
        ),
        name="exchange",
    )(inverse_block, gp, gpt, chosen_rows.reshape(1, -1), panel_a, panel_b)
    return pl.pallas_call(
        final_kernel,
        out_shape=(
            out((OWN, W), F32),
            out((W, W), F32),
            out((OWN, W), F32),
            out((W, W), F32),
            out((W, W), F32),
        ),
        in_specs=[vmem] * 7,
        out_specs=(vmem,) * 5,
        compiler_params=pltpu.CompilerParams(vmem_limit_bytes=48 << 20),
        name="finish",
    )(product_a, product_b, selected, gram, pivot_inverse_a, top_panel_b, pivot_inverse_b)


def solution(mesh):
    in_specs = (P("row", "col"), P(), P("row", "col"), P(), P(), P(), P("row", "col"), P())
    out_specs = (P(("row", "col"), None), P(), P(("row", "col"), None), P(), P())
    return jax.shard_map(body, mesh=mesh, in_specs=in_specs, out_specs=out_specs, check_vma=False)
```

time: 182 us -> 157 us (0.86)
  Pallas kernels: 177 us -> 152 us
    pallas_call x1, Pallas kernels: 171 us -> 146 us  [body(): pl.pallas_call(main_kernel, out_shape=(out((OWN, W), F32), out((OWN, W),...]
where the time goes in v2:
time: 157 us
  Pallas kernels  152 us (97%)
  local copies, waits for them, and re-layouts  4.18 us (3%)
    pallas_call x1, Pallas kernels, body(): pl.pallas_call(main_kernel, out_shape=(out((OWN, W), F32), out((OWN, W),...  146 us
    pallas_call x1, Pallas kernels, body(): pl.pallas_call(final_kernel, out_shape=(out((OWN, W), F32), out((W, W), F...  5.91 us

profile of v2, /device:TPU:1, one launch (start us, length us, event | category | flops | bytes accessed | tf_op | source)
XLA Modules:
  0.0 156.8 jit_solution(11646397051312254872)
XLA Ops:
  0.6 1.5 copy.13
  2.2 0.0 copy-start
  2.2 0.0 copy-start.1
  2.2 0.0 copy-start.2
  2.2 146.1 %exchange.1 = (f32[96,512]{1,0:T(8,128)}, f32[96,512]{1,0:T(8,128)}, f32[96,128]{1,0:T(8,128)}, f32[1536,512]{1,0:T(8,128)}) custom-call(f32[1536,768]{1,0:T(8,128)} %block_ref.1, s32[1,12288]{1,0:T(1,128)} %bitcast.6, s32[128,96]{1,0:T(8,128)} %bitcast.4, s32[1,8192]{1,0:T(1,128)} %bitcast.7, f32[64,768]{1,0:T(8,128)} %pa_ref.1, f32[64,512]{1,0:T(8,128)} %pb_ref.1), custom_call_target="tpu_custom_call" | custom-call | flops 10000000000 | bytes 20000000 | tf_op jit(solution)/shard_map/exchange/pallas_call | solution.py:611
  148.2 0.0 copy-done
  148.3 0.0 copy-done.1
  148.3 0.0 copy-done.2
  148.3 0.0 copy-start.3
  148.3 0.9 copy-done.3
  149.2 0.0 copy-start.4
  149.2 0.9 copy-done.4
  150.1 0.0 copy-start.5
  150.1 0.8 copy-done.5
  150.9 5.9 %finish.1 = (f32[96,512]{1,0:T(8,128)}, f32[512,512]{1,0:T(8,128)}, f32[96,512]{1,0:T(8,128)}, f32[512,512]{1,0:T(8,128)}, f32[512,512]{1,0:T(8,128)}) custom-call(f32[96,512]{1,0:T(8,128)S(1)} %copy-done.3, f32[96,512]{1,0:T(8,128)S(1)} %copy-done.4, f32[96,128]{1,0:T(8,128)S(1)} %copy-done.5, f32[1536,512]{1,0:T(8,128)} %get-tuple-element.12.g_ref, ...), custom_call_target="tpu_custom_call" | custom-call | tf_op jit(solution)/shard_map/finish/pallas_call | solution.py:680
Async XLA Ops:
  2.2 146.1 %copy-start = (f32[512,512]{1,0:T(8,128)S(1)}, f32[512,512]{1,0:T(8,128)}, u32[]{:S(2)}) copy-start(f32[512,512]{1,0:T(8,128)} %pivot_a_ref.1) | copy-start | bytes 3145732
  2.2 146.1 %copy-start.1 = (f32[512,512]{1,0:T(8,128)S(1)}, f32[512,512]{1,0:T(8,128)}, u32[]{:S(2)}) copy-start(f32[512,512]{1,0:T(8,128)} %top_ref.1) | copy-start | bytes 3145732
  2.2 146.1 %copy-start.2 = (f32[512,512]{1,0:T(8,128)S(1)}, f32[512,512]{1,0:T(8,128)}, u32[]{:S(2)}) copy-start(f32[512,512]{1,0:T(8,128)} %pivot_b_ref.1) | copy-start | bytes 3145732
  148.3 0.9 copy-start.3
  149.2 0.9 copy-start.4
  150.1 0.8 copy-start.5

commit v3 on v2

--- a/solution.py
+++ b/solution.py
@@ -11,6 +11,7 @@
 F32 = jnp.float32
 BF16 = jnp.bfloat16
 NT = (((1,), (1,)), ((), ()))
+TN = (((0,), (0,)), ((), ()))
 W = 512
 FEAT = 64
 MA = 768
@@ -29,6 +30,10 @@
 
 def dot_nt(a, b):
     return lax.dot_general(a, b, NT, preferred_element_type=F32)
+
+
+def dot_tn(a, b):
+    return lax.dot_general(a, b, TN, preferred_element_type=F32)
 
 
 def dot3(a, b):
@@ -55,9 +60,6 @@
     chosen_ref,
     pa_ref,
     pb_ref,
-    out_pa_ref,
-    out_pb_ref,
-    out_sel_ref,
     out_g_ref,
     b_f32,
     b_high,
@@ -128,8 +130,9 @@
 
     x_pair = ((1 - x_lo) * 4 + z, c)
     x_across = x_device(2)
-    own_to = (c // 2, (c % 2) * 8 + r)
-    own_from = (c % 8, 2 * r + c // 8)
+    own_part = ((y + z) % 4) * 2 + x_lo
+    own_to = (c // 2, core * 8 + own_part)
+    own_from = (core * 4 + (y + 4 - z) % 4, 2 * r + x_hi)
     own_self = jnp.logical_and(own_to[0] == r, own_to[1] == c)
     pending = []
 
@@ -169,20 +172,19 @@
     steps = (1, 3, 2)
     panels = (pa_ref, pb_ref)
     held = (xa, xb)
-    y_copies = []
-    mate_copies = []
-    for ab in range(2):
-        mate_copies.append(
-            [send(panels[ab], held[ab].at[mine], c_send.at[ab, 0], c_recv.at[ab, 0], mate)]
-        )
-        y_copies.append(
-            [
-                send(
-                    panels[ab], held[ab].at[mine], y_send.at[ab, i], y_recv.at[ab, i], y_device(dy)
-                )
-                for i, dy in enumerate(steps)
-            ]
-        )
+    y_copies = [None, None]
+    mate_copies = [None, None]
+
+    def y_start(ab):
+        mate_copies[ab] = [
+            send(panels[ab], held[ab].at[mine], c_send.at[ab, 0], c_recv.at[ab, 0], mate)
+        ]
+        y_copies[ab] = [
+            send(panels[ab], held[ab].at[mine], y_send.at[ab, i], y_recv.at[ab, i], y_device(dy))
+            for i, dy in enumerate(steps)
+        ]
+
+    y_start(0)
 
     def pass_on(ab, i):
         slot = ((y + 4 - steps[i]) % 4) * 2 + core
@@ -201,7 +203,7 @@
     lax.fori_loop(0, 16, divide, 0)
 
     gpt = gpt_ref[...]
-    table = jnp.concatenate([gpt >> 7, gpt & 127], axis=0).astype(F32).astype(BF16)
+    table = jnp.concatenate([gpt >> 7, gpt & 127], axis=1).astype(F32).T.astype(BF16)
     own_start = r * (OWN * 16) + c * OWN
     tile = 1024
 
@@ -388,21 +390,16 @@
         total = ring_sum(ab, 1)
         ring_copies[ab].wait_recv()
         total = total + x_in[ab]
-        (out_pa_ref, out_pb_ref)[ab][...] = total
+        out_g_ref[pl.ds(3 * W + ab * OWN, OWN), :] = total
         return total
 
     own_copies = []
 
     def own_start_copy(ab):
-        line = lax.broadcasted_iota(jnp.int32, (128, MA), 0)
-        pick = jnp.where(
-            jnp.logical_and(
-                line + r * OWN == lax.broadcasted_iota(jnp.int32, (128, MA), 1), line < OWN
-            ),
-            1.0,
-            0.0,
-        ).astype(BF16)
-        own_out[ab] = dot_nt(full_high[ab], pick) + dot_nt(full_low[ab], pick)
+        line = lax.broadcasted_iota(jnp.int32, (OWN, MA), 0) + own_part * OWN
+        pick = jnp.where(line == lax.broadcasted_iota(jnp.int32, (OWN, MA), 1), 1.0, 0.0)
+        pick = pick.astype(BF16)
+        own_out[ab] = dot_nt(pick, full_high[ab]) + dot_nt(pick, full_low[ab])
         copy = remote(own_out.at[ab], own_in.at[ab], own_send.at[ab], own_recv.at[ab], own_to)
         own_copies.append(copy)
 
@@ -484,34 +481,35 @@
 
     def gram_of(f, p):
         fh, fl = split(f)
-        ph, low = split(jnp.concatenate([p, jnp.zeros((128 - OWN, W), F32)], axis=0))
-        return dot_nn(fh, ph) + (dot_nn(fh, low) + dot_nn(fl, ph))
+        ph, low = split(p)
+        return dot_tn(fh, ph) + (dot_tn(fh, low) + dot_tn(fl, ph))
 
     hits = lax.fori_loop(0, 8192 // tile, place, jnp.zeros((OWN, 128), F32))
-    out_sel_ref[...] = jnp.broadcast_to(jnp.sum(hits, axis=1, keepdims=True), (OWN, 128))
+    out_g_ref[pl.ds(3 * W + 2 * OWN, OWN), :] = jnp.broadcast_to(jnp.sum(hits, axis=1, keepdims=True), (OWN, W))
     far_a = gather_far(0)
+    y_start(1)
     gather_near(0)
-    for i in range(3):
-        pass_on(1, i)
     far_a.wait_recv()
     near[0] += far_in[0]
     row_start(0)
+    for i in range(3):
+        pass_on(1, i)
     far_b = gather_far(1)
     row_turn(0, 0)
     gather_near(1)
     far_b.wait_recv()
     near[1] += far_in[1]
+    row_turn(0, 1)
     row_start(1)
-    row_turn(0, 1)
-    row_turn(1, 0)
     row_end(0)
     product_out(0, 0)
+    row_turn(1, 0)
     product_out(0, 1)
     product_own(0, 0)
     ring_start(0, 0)
+    row_turn(1, 1)
     product_own(0, 1)
     ring_start(0, 1)
-    row_turn(1, 1)
     own_start_copy(0)
     ring_turn(0, 0)
     ring_turn(0, 1)
@@ -575,12 +573,14 @@
 
 
 def final_kernel(
-    pa_ref, pb_ref, sel_ref, g_ref, pivot_a_ref, top_ref, pivot_b_ref, ia_ref, da_ref, ib_ref, tb_ref, db_ref
+    g_ref, pivot_a_ref, top_ref, pivot_b_ref, ia_ref, da_ref, ib_ref, tb_ref, db_ref
 ):
     top = top_ref[...]
-    product_a = pa_ref[...]
+    product_a = g_ref[3 * W : 3 * W + OWN, :]
+    product_b = g_ref[3 * W + OWN : 3 * W + 2 * OWN, :]
+    selected = g_ref[3 * W + 2 * OWN :, :]
     ia_ref[...] = -product_a
-    ib_ref[...] = -(pb_ref[...] - dot3(product_a, top)) * sel_ref[:, :1]
+    ib_ref[...] = -(product_b - dot3(product_a, top)) * selected
     diagonal_a = pivot_a_ref[...] + g_ref[:W, :]
     da_ref[...] = diagonal_a
     cross_neg_t = g_ref[W : 2 * W, :]
@@ -589,7 +589,7 @@
     tb_ref[...] = top_b
     top_t = top.T
     db_ref[...] = (
-        pivot_b_ref[...] - dot3(top_t, top_b) + (g_ref[2 * W :, :] - dot3(cross_neg_t, top))
+        pivot_b_ref[...] - dot3(top_t, top_b) + (g_ref[2 * W : 3 * W, :] - dot3(cross_neg_t, top))
     )
 
 
@@ -607,17 +607,12 @@
     dma = pltpu.SemaphoreType.DMA
     out = jax.ShapeDtypeStruct
     gp = grid_position.reshape(1, -1)
-    gpt = grid_position.reshape(96, 128).T
-    product_a, product_b, selected, gram = pl.pallas_call(
+    gpt = grid_position.reshape(96, 128)
+    gram = pl.pallas_call(
         main_kernel,
-        out_shape=(
-            out((OWN, W), F32),
-            out((OWN, W), F32),
-            out((OWN, 128), F32),
-            out((3 * W, W), F32),
-        ),
+        out_shape=out((3 * W + 3 * OWN, W), F32),
         in_specs=[pl.BlockSpec(memory_space=pl.ANY)] + [vmem] * 5,
-        out_specs=(vmem,) * 4,
+        out_specs=vmem,
         scratch_shapes=[
             pltpu.VMEM((1536, MA), F32),
             pltpu.VMEM((2, 768, MA), BF16),
@@ -638,8 +633,8 @@
             pltpu.VMEM((2, 2, 2, OWN, W), F32),
             pltpu.VMEM((2, OWN, W), F32),
             pltpu.VMEM((2, OWN, W), F32),
-            pltpu.VMEM((2, W, 128), F32),
-            pltpu.VMEM((2, W, 128), F32),
+            pltpu.VMEM((2, OWN, W), F32),
+            pltpu.VMEM((2, OWN, W), F32),
             pltpu.VMEM((3 * W, W), F32),
             pltpu.VMEM((3 * W // 2, W), F32),
             pltpu.VMEM((4, 3, 64, W), F32),
@@ -686,11 +681,11 @@
             out((W, W), F32),
             out((W, W), F32),
         ),
-        in_specs=[vmem] * 7,
+        in_specs=[vmem] * 4,
         out_specs=(vmem,) * 5,
         compiler_params=pltpu.CompilerParams(vmem_limit_bytes=48 << 20),
         name="finish",
-    )(product_a, product_b, selected, gram, pivot_inverse_a, top_panel_b, pivot_inverse_b)
+    )(gram, pivot_inverse_a, top_panel_b, pivot_inverse_b)
 
 
 def solution(mesh):

time: 157 us -> 147 us (0.936)
  Pallas kernels: 152 us -> 147 us
  local copies, waits for them, and re-layouts: 4.18 us -> 0.01 us
    pallas_call x1, Pallas kernels: 146 us -> 141 us  [body(): pl.pallas_call(main_kernel, out_shape=out((3 * W + 3 * OWN, W), F32), in_...]
    unnamed x12 -> x6, local copies, waits for them, and re-layouts: 2.66 us -> 0.01 us
where the time goes in v3:
time: 147 us
  Pallas kernels  147 us (100%)
    pallas_call x1, Pallas kernels, body(): pl.pallas_call(main_kernel, out_shape=out((3 * W + 3 * OWN, W), F32), in_...  141 us
    pallas_call x1, Pallas kernels, body(): pl.pallas_call(final_kernel, out_shape=(out((OWN, W), F32), out((W, W), F...  6.01 us

profile of v3, /device:TPU:1, one launch (start us, length us, event | category | flops | bytes accessed | tf_op | source)
XLA Modules:
  0.0 147.3 jit_solution(13242829160529452854)
XLA Ops:
  0.6 0.0 copy-start
  0.6 0.0 copy-start.1
  0.7 0.0 copy-start.2
  0.7 140.6 %exchange.1.g_ref = f32[1824,512]{1,0:T(8,128)} custom-call(f32[1536,768]{1,0:T(8,128)} %block_ref.1, s32[1,12288]{1,0:T(1,128)} %bitcast.3, s32[96,128]{1,0:T(8,128)} %bitcast.4, s32[1,8192]{1,0:T(1,128)} %bitcast.5, f32[64,768]{1,0:T(8,128)} %pa_ref.1, f32[64,512]{1,0:T(8,128)} %pb_ref.1), custom_call_target="tpu_custom_call" | custom-call | flops 10000000000 | bytes 20000000 | tf_op jit(solution)/shard_map/exchange/pallas_call | solution.py:611
  141.2 0.0 copy-done
  141.2 0.0 copy-done.1
  141.3 0.0 copy-done.2
  141.3 6.0 %finish.1 = (f32[96,512]{1,0:T(8,128)}, f32[512,512]{1,0:T(8,128)}, f32[96,512]{1,0:T(8,128)}, f32[512,512]{1,0:T(8,128)}, f32[512,512]{1,0:T(8,128)}) custom-call(f32[1824,512]{1,0:T(8,128)} %exchange.1.g_ref, f32[512,512]{1,0:T(8,128)S(1)} %copy-done, f32[512,512]{1,0:T(8,128)S(1)} %copy-done.1, f32[512,512]{1,0:T(8,128)S(1)} %copy-done.2), custom_call_target="tpu_custom_call" | custom-call | tf_op jit(solution)/shard_map/finish/pallas_call | solution.py:675
Async XLA Ops:
  0.6 140.6 %copy-start = (f32[512,512]{1,0:T(8,128)S(1)}, f32[512,512]{1,0:T(8,128)}, u32[]{:S(2)}) copy-start(f32[512,512]{1,0:T(8,128)} %pivot_a_ref.1) | copy-start | bytes 3145732
  0.6 140.6 %copy-start.1 = (f32[512,512]{1,0:T(8,128)S(1)}, f32[512,512]{1,0:T(8,128)}, u32[]{:S(2)}) copy-start(f32[512,512]{1,0:T(8,128)} %top_ref.1) | copy-start | bytes 3145732
  0.7 140.6 %copy-start.2 = (f32[512,512]{1,0:T(8,128)S(1)}, f32[512,512]{1,0:T(8,128)}, u32[]{:S(2)}) copy-start(f32[512,512]{1,0:T(8,128)} %pivot_b_ref.1) | copy-start | bytes 3145732

commit v4 on v3

--- a/solution.py
+++ b/solution.py
@@ -82,6 +82,7 @@
     x_in,
     own_out,
     own_in,
+    own_far,
     gram,
     gram_core,
     gram_1,
@@ -106,6 +107,8 @@
     own_recv,
     gc_send,
     gc_recv,
+    of_send,
+    of_recv,
     gs_send,
     gs_recv,
     gg_send,
@@ -386,8 +389,9 @@
             x_out.at[ab], x_in.at[ab], x_send.at[ab], x_recv.at[ab], x_across
         )
 
-    def ring_end(ab):
-        total = ring_sum(ab, 1)
+    def ring_end(ab, total=None):
+        if total is None:
+            total = ring_sum(ab, 1)
         ring_copies[ab].wait_recv()
         total = total + x_in[ab]
         out_g_ref[pl.ds(3 * W + ab * OWN, OWN), :] = total
@@ -525,9 +529,10 @@
     product_a = ring_end(0)
     ring_turn(1, 0)
     ring_turn(1, 1)
+    own_wait(1)
+    own_across = send(own_in.at[1], own_far, of_send, of_recv, x_across)
     own_wait(0)
     gram[0:W, :] = gram_of(own_in[0], product_a)
-    own_wait(1)
     gram[W : 2 * W, :] = gram_of(own_in[1], product_a)
     core_a = send(
         gram.at[rows_of((1 - core) * W, W), :],
@@ -536,15 +541,17 @@
         gc_recv.at[0],
         mate,
     )
+    ring_across(1)
     core_a.wait_recv()
     gram_core[0:W, :] += gram[rows_of(core * W, W), :]
     gram_step(0, 0)
     gram_step(1, 0)
-    ring_across(1)
-    gram_step(0, 1)
-    gram_step(1, 1)
-    product_b = ring_end(1)
-    gram[2 * W : 3 * W, :] = gram_of(own_in[1], product_b)
+    total_b = ring_sum(1, 1)
+    own_across.wait_recv()
+    gram[2 * W : 3 * W, :] = gram_of(
+        jnp.concatenate([own_in[1], own_far[...]], axis=0),
+        jnp.concatenate([total_b, x_out[1]], axis=0),
+    )
     core_b = send(
         gram.at[rows_of(2 * W + (1 - core) * 256, 256), :],
         gram_core.at[W : W + 256, :],
@@ -552,20 +559,35 @@
         gc_recv.at[1],
         mate,
     )
-    gram_step(0, 2)
-    gram_step(1, 2)
     core_b.wait_recv()
     gram_core[W : W + 256, :] += gram[rows_of(2 * W + core * 256, 256), :]
     gram_step(2, 0)
     gram_step(3, 0)
+    gram_step(2, 1)
+    gram_step(3, 1)
+    ring_end(1, total_b)
+    gram_step(0, 1)
+    gram_step(1, 1)
+    gram_step(2, 2)
+    gram_step(3, 2)
+    gram_step(0, 2)
+    gram_step(1, 2)
+    gram_step(2, 3)
+    gram_step(3, 3)
     gram_step(0, 3)
     gram_step(1, 3)
-    for n in range(1, 7):
-        gram_step(2, n)
-        gram_step(3, n)
-        if n + 3 < 7:
-            gram_step(0, n + 3)
-            gram_step(1, n + 3)
+    gram_step(2, 4)
+    gram_step(3, 4)
+    gram_step(0, 4)
+    gram_step(1, 4)
+    gram_step(2, 5)
+    gram_step(3, 5)
+    gram_step(0, 5)
+    gram_step(1, 5)
+    gram_step(2, 6)
+    gram_step(3, 6)
+    gram_step(0, 6)
+    gram_step(1, 6)
     for p in range(4):
         gram_copies[p, 6][0].wait_recv()
     for copy in pending:
@@ -635,6 +657,7 @@
             pltpu.VMEM((2, OWN, W), F32),
             pltpu.VMEM((2, OWN, W), F32),
             pltpu.VMEM((2, OWN, W), F32),
+            pltpu.VMEM((OWN, W), F32),
             pltpu.VMEM((3 * W, W), F32),
             pltpu.VMEM((3 * W // 2, W), F32),
             pltpu.VMEM((4, 3, 64, W), F32),
@@ -659,6 +682,8 @@
             dma((2,)),
             dma((2,)),
             dma((2,)),
+            dma,
+            dma,
             dma((4, 6, 3)),
             dma((4, 6, 3)),
             dma((4,)),

time: 147 us -> 140 us (0.952)
  Pallas kernels: 147 us -> 139 us
    pallas_call x1, Pallas kernels: 141 us -> 133 us  [body(): pl.pallas_call(main_kernel, out_shape=out((3 * W + 3 * OWN, W), F32), in_...]
where the time goes in v4:
time: 140 us
  Pallas kernels  139 us (99%)
    pallas_call x1, Pallas kernels, body(): pl.pallas_call(main_kernel, out_shape=out((3 * W + 3 * OWN, W), F32), in_...  133 us
    pallas_call x1, Pallas kernels, body(): pl.pallas_call(final_kernel, out_shape=(out((OWN, W), F32), out((W, W), F...  6.01 us

profile of v4, /device:TPU:1, one launch (start us, length us, event | category | flops | bytes accessed | tf_op | source)
XLA Modules:
  0.0 140.2 jit_solution(4609546331964487633)
XLA Ops:
  0.6 0.0 copy-start
  0.6 0.0 copy-start.1
  0.7 0.0 copy-start.2
  0.7 133.5 %exchange.1.g_ref = f32[1824,512]{1,0:T(8,128)} custom-call(f32[1536,768]{1,0:T(8,128)} %block_ref.1, s32[1,12288]{1,0:T(1,128)} %bitcast.3, s32[96,128]{1,0:T(8,128)} %bitcast.4, s32[1,8192]{1,0:T(1,128)} %bitcast.5, f32[64,768]{1,0:T(8,128)} %pa_ref.1, f32[64,512]{1,0:T(8,128)} %pb_ref.1), custom_call_target="tpu_custom_call" | custom-call | flops 10000000000 | bytes 20000000 | tf_op jit(solution)/shard_map/exchange/pallas_call | solution.py:633
  134.1 0.0 copy-done
  134.1 0.0 copy-done.1
  134.2 0.0 copy-done.2
  134.2 6.0 %finish.1 = (f32[96,512]{1,0:T(8,128)}, f32[512,512]{1,0:T(8,128)}, f32[96,512]{1,0:T(8,128)}, f32[512,512]{1,0:T(8,128)}, f32[512,512]{1,0:T(8,128)}) custom-call(f32[1824,512]{1,0:T(8,128)} %exchange.1.g_ref, f32[512,512]{1,0:T(8,128)S(1)} %copy-done, f32[512,512]{1,0:T(8,128)S(1)} %copy-done.1, f32[512,512]{1,0:T(8,128)S(1)} %copy-done.2), custom_call_target="tpu_custom_call" | custom-call | tf_op jit(solution)/shard_map/finish/pallas_call | solution.py:700
Async XLA Ops:
  0.6 133.5 %copy-start = (f32[512,512]{1,0:T(8,128)S(1)}, f32[512,512]{1,0:T(8,128)}, u32[]{:S(2)}) copy-start(f32[512,512]{1,0:T(8,128)} %pivot_a_ref.1) | copy-start | bytes 3145732
  0.6 133.5 %copy-start.1 = (f32[512,512]{1,0:T(8,128)S(1)}, f32[512,512]{1,0:T(8,128)}, u32[]{:S(2)}) copy-start(f32[512,512]{1,0:T(8,128)} %top_ref.1) | copy-start | bytes 3145732
  0.7 133.5 %copy-start.2 = (f32[512,512]{1,0:T(8,128)S(1)}, f32[512,512]{1,0:T(8,128)}, u32[]{:S(2)}) copy-start(f32[512,512]{1,0:T(8,128)} %pivot_b_ref.1) | copy-start | bytes 3145732

commit v5 on v4

--- a/solution.py
+++ b/solution.py
@@ -258,6 +258,8 @@
             base = ((y + 4 - dy) % 4) * 2
             if ab == 0:
                 pass_on(ab, i)
+            if ab == 0 and i == 2:
+                y_start(1)
             gather(ab, base + core, far, 1 - x_hi)
             mate_copies[ab][i + 1].wait_recv()
             gather(ab, base + 1 - core, far, 1 - x_hi)
@@ -297,15 +299,16 @@
         base = sets[s] * 4
         below = base + (z + 3) % 4
         above = base + (z + 1) % 4
+        if s == 0:
+            other = (1 - x_lo) * 4 + z
+            row_copies[ab]["pair"].wait_recv()
+            row_put(ab, "up1", None, other, None, 5, z_device(1))
+            row_put(ab, "down1", None, other, None, 6, z_device(3))
         row_copies[ab]["up%d" % s].wait_recv()
         row_put(ab, "far_up%d" % s, None, below, 0, 3 + 4 * s, z_device(1))
         row_copies[ab]["down%d" % s].wait_recv()
         row_put(ab, "far_down%d" % s, None, above, 1, 4 + 4 * s, z_device(3))
         if s == 0:
-            other = (1 - x_lo) * 4 + z
-            row_copies[ab]["pair"].wait_recv()
-            row_put(ab, "up1", None, other, None, 5, z_device(1))
-            row_put(ab, "down1", None, other, None, 6, z_device(3))
             store_full(ab, other, full[ab, other])
         store_full(ab, below, full[ab, below])
         store_full(ab, above, full[ab, above])
@@ -491,7 +494,6 @@
     hits = lax.fori_loop(0, 8192 // tile, place, jnp.zeros((OWN, 128), F32))
     out_g_ref[pl.ds(3 * W + 2 * OWN, OWN), :] = jnp.broadcast_to(jnp.sum(hits, axis=1, keepdims=True), (OWN, W))
     far_a = gather_far(0)
-    y_start(1)
     gather_near(0)
     far_a.wait_recv()
     near[0] += far_in[0]

time: 140 us -> 139 us (level)
  no operation moved by 1% of the time
where the time goes in v5:
time: 139 us
  Pallas kernels  138 us (99%)
    pallas_call x1, Pallas kernels, body(): pl.pallas_call(main_kernel, out_shape=out((3 * W + 3 * OWN, W), F32), in_...  132 us
    pallas_call x1, Pallas kernels, body(): pl.pallas_call(final_kernel, out_shape=(out((OWN, W), F32), out((W, W), F...  6.02 us

profile of v5, /device:TPU:1, one launch (start us, length us, event | category | flops | bytes accessed | tf_op | source)
XLA Modules:
  0.0 139.0 jit_solution(7205039584766944627)
XLA Ops:
  0.6 0.0 copy-start
  0.6 0.0 copy-start.1
  0.7 0.0 copy-start.2
  0.7 132.2 %exchange.1.g_ref = f32[1824,512]{1,0:T(8,128)} custom-call(f32[1536,768]{1,0:T(8,128)} %block_ref.1, s32[1,12288]{1,0:T(1,128)} %bitcast.3, s32[96,128]{1,0:T(8,128)} %bitcast.4, s32[1,8192]{1,0:T(1,128)} %bitcast.5, f32[64,768]{1,0:T(8,128)} %pa_ref.1, f32[64,512]{1,0:T(8,128)} %pb_ref.1), custom_call_target="tpu_custom_call" | custom-call | flops 10000000000 | bytes 20000000 | tf_op jit(solution)/shard_map/exchange/pallas_call | solution.py:635
  132.9 0.0 copy-done
  132.9 0.0 copy-done.1
  132.9 0.0 copy-done.2
  132.9 6.0 %finish.1 = (f32[96,512]{1,0:T(8,128)}, f32[512,512]{1,0:T(8,128)}, f32[96,512]{1,0:T(8,128)}, f32[512,512]{1,0:T(8,128)}, f32[512,512]{1,0:T(8,128)}) custom-call(f32[1824,512]{1,0:T(8,128)} %exchange.1.g_ref, f32[512,512]{1,0:T(8,128)S(1)} %copy-done, f32[512,512]{1,0:T(8,128)S(1)} %copy-done.1, f32[512,512]{1,0:T(8,128)S(1)} %copy-done.2), custom_call_target="tpu_custom_call" | custom-call | tf_op jit(solution)/shard_map/finish/pallas_call | solution.py:702
Async XLA Ops:
  0.6 132.3 %copy-start = (f32[512,512]{1,0:T(8,128)S(1)}, f32[512,512]{1,0:T(8,128)}, u32[]{:S(2)}) copy-start(f32[512,512]{1,0:T(8,128)} %pivot_a_ref.1) | copy-start | bytes 3145732
  0.6 132.3 %copy-start.1 = (f32[512,512]{1,0:T(8,128)S(1)}, f32[512,512]{1,0:T(8,128)}, u32[]{:S(2)}) copy-start(f32[512,512]{1,0:T(8,128)} %top_ref.1) | copy-start | bytes 3145732
  0.7 132.3 %copy-start.2 = (f32[512,512]{1,0:T(8,128)S(1)}, f32[512,512]{1,0:T(8,128)}, u32[]{:S(2)}) copy-start(f32[512,512]{1,0:T(8,128)} %pivot_b_ref.1) | copy-start | bytes 3145732
